TPU v7x, 32 devices: a whole 2x2x4 slice. The times are simulated.
32 devices in a mesh: grp: 4 (over y, x), seq: 8 (over z, core).
Axes of the slice: x: 2, y: 2, z: 4, core: 2. Of those that a mesh axis runs over, the one named last changes fastest.
Arguments:
- query_input: bfloat16 [4096, 4096], P(('grp', 'seq')), may hold values from -8 to 8
- key_input: bfloat16 [4096, 512], P(('grp', 'seq')), may hold values from -8 to 8
- value_input: bfloat16 [4096, 512], P(('grp', 'seq')), may hold values from -6 to 6
- out_grad: bfloat16 [4096, 4096], P(('grp', 'seq')), may hold values from -6 to 6
- key_blocks: int32 [32, 12], replicated, may hold values from 0 to 31, as said below
- key_counts: int32 [32], replicated, may hold values from 1 to 12, as said below
- block_position: int32 [32], replicated, may hold values from 0 to 31, each once
Outputs:
- attn_out: bfloat16 [4096, 4096], P(('grp', 'seq'))
- query_grad: bfloat16 [4096, 4096], P(('grp', 'seq'))
- key_grad: bfloat16 [4096, 512], P(('grp', 'seq'))
- value_grad: bfloat16 [4096, 512], P(('grp', 'seq'))
Inputs may be any that keep to these rules, and one draw needn't show every extreme that they name: `key_blocks`: in row b the first key_counts[b] entries are distinct, the first is b itself and the others are earlier blocks of the same group of 8 blocks or of the group before; the remaining entries equal b. `key_counts`: the last block's count is 12.
All inputs are finite; a program needn't handle non-finite values.
Results may differ from a plain program's by a relative error of at most 0.015.
Values may be sent and summed in bfloat16 or wider, within the bound.
No kernel may reach another device: no remote copies, remote signals or barrier semaphores. Data moves between devices by JAX's collectives and lax.ppermute only.
A program may use at most 128 MiB of HBM per device.

v0:
```python
import functools
import math

import jax
import jax.numpy as jnp
import numpy as np
from jax import lax
from jax.experimental import pallas as pl
from jax.experimental.pallas import tpu as pltpu
from jax.sharding import PartitionSpec as P

HEADS = 32
KV_HEADS = 4
HEAD_DIM = 128
BLK = 128
CORES = 2
RATIO = HEADS // KV_HEADS
HALF_KV = KV_HEADS // CORES
ROWS = RATIO * BLK
SCALE = 1.0 / math.sqrt(HEAD_DIM)
TO_LOG2 = SCALE * math.log2(math.e)
F32 = jnp.float32
BF16 = jnp.bfloat16
CHUNK = 256

VMEM_SPEC = pl.BlockSpec(memory_space=pltpu.VMEM)
HBM_SPEC = pl.BlockSpec(memory_space=pltpu.HBM)
SMEM_SPEC = pl.BlockSpec(memory_space=pltpu.SMEM)


def trig_table(n_blocks):
    half = HEAD_DIM // 2
    frequency = np.power(500000.0, -np.arange(half) * (2.0 / HEAD_DIM))
    parts = []
    for places in (np.arange(n_blocks) * BLK, np.arange(BLK)):
        angles = places[:, None] * frequency
        for part in (np.cos(angles), np.sin(angles)):
            parts.append(np.concatenate([part, part], axis=1))
    return np.concatenate(parts, axis=0).astype(np.float32)


def block_tables(place, table):
    n_blocks = table.shape[0] // 2 - BLK
    cos_b = table[pl.ds(place, 1), :]
    sin_b = table[pl.ds(n_blocks + place, 1), :]
    cos_t = table[2 * n_blocks : 2 * n_blocks + BLK, :]
    sin_t = table[2 * n_blocks + BLK :, :]
    cosine = cos_b * cos_t - sin_b * sin_t
    sine = sin_b * cos_t + cos_b * sin_t
    lanes = lax.broadcasted_iota(jnp.int32, sine.shape, 1)
    return cosine, jnp.where(lanes < HEAD_DIM // 2, -sine, sine)


def turn(values, cosine, signed_sine):
    return values * cosine + pltpu.roll(values, HEAD_DIM // 2, 1) * signed_sine


def dot_nt(a, b):
    return lax.dot_general(a, b, (((1,), (1,)), ((), ())), preferred_element_type=F32)


def dot_nn(a, b):
    return lax.dot_general(a, b, (((1,), (0,)), ((), ())), preferred_element_type=F32)


def here(n_seq):
    member = lax.axis_index("seq")
    group = lax.axis_index("grp")
    return group, member, lax.rem(member, CORES)


def size_of(array):
    return math.prod(array.shape) * jnp.dtype(array.dtype).itemsize


def call(kernel, out_shape, n_smem, scratch=(), us=1, name=None, n_hbm=0, hbm_out=None, hold=()):
    def placed(n, a):
        if n == hbm_out:
            return pltpu.HBM(a.shape, a.dtype)
        return a

    def spec(n, a):
        if a.dtype == jnp.int32:
            return SMEM_SPEC
        return HBM_SPEC if n == hbm_out else VMEM_SPEC

    def run(*arrays):
        n_left = n_smem + n_hbm
        outs = list(out_shape) if isinstance(out_shape, (tuple, list)) else [out_shape]
        held = sum(size_of(a) for a in arrays[n_left:])
        held += sum(size_of(a) for n, a in enumerate(outs) if n != hbm_out)
        held += sum(size_of(a) for a in scratch if a.dtype in (F32, BF16))
        in_specs = [SMEM_SPEC] * n_smem + [HBM_SPEC] * n_hbm
        in_specs += [VMEM_SPEC] * (len(arrays) - n_left)
        pinned = [
            pltpu.with_memory_space_constraint(a, pltpu.HBM) if n < n_left or n in hold else a
            for n, a in enumerate(arrays)
        ]
        results = pl.pallas_call(
            kernel,
            out_shape=[placed(n, a) for n, a in enumerate(outs)],
            in_specs=in_specs,
            out_specs=[spec(n, a) for n, a in enumerate(outs)],
            scratch_shapes=list(scratch),
            compiler_params=pltpu.CompilerParams(vmem_limit_bytes=held + 6 * 2**20),
            cost_estimate=pl.CostEstimate(
                flops=us * 10**9, bytes_accessed=2**20, transcendentals=0
            ),
            name=name,
        )(*pinned)
        return results if isinstance(out_shape, (tuple, list)) else results[0]

    return run


def prepare(n_seq, place_ref, *refs):
    key, value, query, grad, table_hbm, kv_keep, kv_send, q_keep, q_send = refs[:9]
    key_here, value_here, table, query_here, grad_here, kept, sems = refs[9:]
    group, member, core = here(n_seq)
    half_heads = HEADS // CORES
    halves = (1 - core, core)

    def copy(n, source, place):
        return pltpu.make_async_copy(source, place, sems.at[n])

    def columns(first, count=1):
        return pl.ds(pl.multiple_of(first * HEAD_DIM, HEAD_DIM), count * HEAD_DIM)

    loads = [copy(0, key, key_here), copy(1, table_hbm, table), copy(2, value, value_here)]
    for n, half in enumerate(halves):
        part = columns(half * half_heads, half_heads)
        loads.append(copy(3 + 2 * n, query.at[:, part], query_here.at[n]))
        loads.append(copy(4 + 2 * n, grad.at[:, part], grad_here.at[n]))
    for load in (*loads[:3], *loads[5:], *loads[3:5]):
        load.start()
    for load in loads[:3]:
        load.wait()
    cosine, sine = block_tables(place_ref[group * n_seq + member], table)
    for half, out in zip(halves, (kv_send, kv_keep)):
        for h in range(HALF_KV):
            at = columns(half * HALF_KV + h)
            out[0, h] = turn(key_here[:, at].astype(F32), cosine, sine).astype(BF16)
            out[1, h] = value_here[:, at]
    away = copy(7, kept, q_keep)
    for n, out in ((1, kept), (0, q_send)):
        loads[3 + 2 * n].wait()
        loads[4 + 2 * n].wait()
        for h in range(HALF_KV):
            for r in range(RATIO):
                at = slice((h * RATIO + r) * HEAD_DIM, (h * RATIO + r + 1) * HEAD_DIM)
                part = query_here[n, :, at].astype(F32)
                out[0, h, r] = turn(part, cosine, sine).astype(BF16)
                out[1, h, r] = grad_here[n, :, at]
        if n == 1:
            away.start()
    away.wait()


def make_lists(n_seq, split, key_blocks, key_counts, lists, counts):
    group, member, _ = here(n_seq)
    for i in range(2):
        block = group * n_seq + lax.bitwise_xor(member, i)
        for section in range(3):
            counts[i, section] = int(section == 1)
        lists[i, 1, 0] = i

        def look(j, _):
            place = lax.bitwise_xor(key_blocks[block, j] - (group - 1) * n_seq, member)
            section = (place >= n_seq).astype(jnp.int32)
            section += (place >= n_seq + split).astype(jnp.int32)
            n = counts[i, section]
            lists[i, section, n] = place - jnp.where(section == 0, 0, n_seq) - jnp.where(
                section == 2, split, 0
            )
            counts[i, section] = n + 1
            return 0

        lax.fori_loop(1, key_counts[block], look, 0)
        total = 0
        for section, base in enumerate((0, n_seq, n_seq + split)):

            def append(n, m):
                lists[i, 3, m] = lists[i, section, n] + base
                return m + 1

            total = lax.fori_loop(0, counts[i, section], append, jnp.int32(total))
        counts[i, 3] = total
        lists[i, 3, total] = 0


def causal():
    keys = lax.broadcasted_iota(jnp.int32, (BLK, CHUNK), 0)
    tokens = lax.rem(lax.broadcasted_iota(jnp.int32, (BLK, CHUNK), 1), BLK)
    return keys <= tokens


def chunks():
    per = CHUNK // BLK
    return [
        (slice(c * per, (c + 1) * per), slice(c * CHUNK, (c + 1) * CHUNK))
        for c in range(ROWS // CHUNK)
    ]


def heads_of(block, what, h, rows):
    return block[what, h, rows].reshape(CHUNK, HEAD_DIM)


def fill(store, pieces, first=0):
    for k, piece in enumerate(pieces):
        store[first + CORES * k : first + CORES * (k + 1)] = piece[...]


def pair_scores(store, e, h, block, rows, diagonal):
    scores = dot_nt(store[e, 0, h], heads_of(block, 0, h, rows))
    if diagonal:
        scores = jnp.where(causal(), scores, -1e30)
    return scores, dot_nt(store[e, 1, h], heads_of(block, 1, h, rows))


def gather_stats(store, e, block, stats, i, diagonal, kept=None):
    for h in range(HALF_KV):
        for rows, columns in chunks():
            scores, dprobs = pair_scores(store, e, h, block, rows, diagonal)
            if kept is not None:
                n, kept_scores, kept_dprobs = kept
                kept_scores[n, h, :, columns] = scores
                kept_dprobs[n, h, :, columns] = dprobs
            top = jnp.max(scores, axis=0, keepdims=True)
            if not diagonal:
                old_top = stats[i, h, 0:1, columns]
                top = jnp.maximum(top, old_top)
            weights = jnp.exp2((scores - top) * TO_LOG2)
            total = jnp.sum(weights, axis=0, keepdims=True)
            mixed = jnp.sum(weights * dprobs, axis=0, keepdims=True)
            if not diagonal:
                shrink = jnp.exp2((old_top - top) * TO_LOG2)
                total += stats[i, h, 1:2, columns] * shrink
                mixed += stats[i, h, 2:3, columns] * shrink
            stats[i, h, 0:1, columns] = top
            stats[i, h, 1:2, columns] = total
            stats[i, h, 2:3, columns] = mixed


def spread_grads(found, count, kept_scores, kept_dprobs, stats, i, block, acc, saved, low, sent):
    def copy(n):
        return pltpu.make_async_copy(low.at[n], saved.at[i, n], sent.at[n])

    def add(n, _):
        e = found[n]
        for h in range(HALF_KV):
            dk, dv = acc[e, 0, h], acc[e, 1, h]
            for rows, columns in chunks():
                probs = jnp.exp2(
                    kept_scores[n, h, :, columns] * TO_LOG2 - stats[i, h, 0:1, columns]
                )
                dscores = probs * (kept_dprobs[n, h, :, columns] - stats[i, h, 2:3, columns])
                probs, dscores = probs.astype(BF16), dscores.astype(BF16)
                low[n, h, 0, :, columns] = probs
                low[n, h, 1, :, columns] = dscores
                dv += dot_nn(probs, heads_of(block, 1, h, rows))
                dk += dot_nn(dscores, heads_of(block, 0, h, rows))
            acc[e, 0, h] = dk
            acc[e, 1, h] = dv
        copy(n).start()
        return 0

    def finish(n, _):
        copy(n).wait()
        return 0

    lax.fori_loop(0, count, add, 0)
    lax.fori_loop(0, count, finish, 0)


def write_grads(acc, outs):
    start = 0
    for out in outs:
        part = slice(start, start + out.shape[0])
        out[:, 0] = (acc[part, 0] * SCALE).astype(out.dtype)
        out[:, 1] = acc[part, 1].astype(out.dtype)
        start += out.shape[0]


def current_stats(section, lists, counts, own, other, *rest):
    *pieces, stats, store = rest
    first = section == 1
    if not first:
        stats_in, *pieces = pieces
        stats[...] = stats_in[...]
    fill(store, pieces)
    for i, block in enumerate((own, other)):
        if first:
            gather_stats(store, i, block, stats, i, True)

        def step(n, _):
            gather_stats(store, lists[i, section, n], block, stats, i, False)
            return 0

        lax.fori_loop(int(first), counts[i, section], step, 0)


def previous_grads(n_pieces, lists, counts, own, other, stats_in, *rest):
    n_ends = 2 * n_pieces - 1
    pieces, outs = rest[:n_pieces], rest[n_pieces:n_ends]
    saved, stats, store, acc, low, sent, kept_scores, kept_dprobs = rest[n_ends:]
    fill(store, pieces)
    acc[...] = jnp.zeros_like(acc)
    stats[...] = stats_in[...]
    for i, block in enumerate((own, other)):
        count = counts[i, 0]

        def look(n, _):
            gather_stats(
                store, lists[i, 0, n], block, stats, i, False, (n, kept_scores, kept_dprobs)
            )
            return 0

        lax.fori_loop(0, count, look, 0)
        for h in range(HALF_KV):
            total = stats[i, h, 1:2, :]
            stats[i, h, 0:1, :] = stats[i, h, 0:1, :] * TO_LOG2 + jnp.log2(total)
            stats[i, h, 2:3, :] = stats[i, h, 2:3, :] / total

        def copy(n):
            return pltpu.make_async_copy(low.at[n], saved.at[i, n], sent.at[n])

        def add(n, _):
            e = lists[i, 0, n]
            for h in range(HALF_KV):
                dk, dv = acc[e, 0, h], acc[e, 1, h]
                for rows, columns in chunks():
                    probs = jnp.exp2(
                        kept_scores[n, h, :, columns] * TO_LOG2 - stats[i, h, 0:1, columns]
                    )
                    dscores = probs * (kept_dprobs[n, h, :, columns] - stats[i, h, 2:3, columns])
                    probs, dscores = probs.astype(BF16), dscores.astype(BF16)
                    low[n, h, 0, :, columns] = probs
                    low[n, h, 1, :, columns] = dscores
                    dv += dot_nn(probs, heads_of(block, 1, h, rows))
                    dk += dot_nn(dscores, heads_of(block, 0, h, rows))
                acc[e, 0, h] = dk
                acc[e, 1, h] = dv
            copy(n).start()
            return 0

        def finish(n, _):
            copy(n).wait()
            return 0

        lax.fori_loop(0, count, add, 0)
        lax.fori_loop(0, count, finish, 0)
    write_grads(acc, outs)


def current_grads(section, n_pieces, lists, counts, own, other, stats, *rest):
    pieces, outs = rest[:n_pieces], rest[n_pieces : 2 * n_pieces]
    saved, store, acc, low, sent = rest[2 * n_pieces :]
    first = section == 1
    fill(store, pieces)
    acc[...] = jnp.zeros_like(acc)
    for i, block in enumerate((own, other)):
        count = counts[i, section]

        def copy(n):
            return pltpu.make_async_copy(low.at[n], saved.at[i, n], sent.at[n])

        def look(n, diagonal):
            e = lists[i, section, n]
            for h in range(HALF_KV):
                for rows, columns in chunks():
                    scores, dprobs = pair_scores(store, e, h, block, rows, diagonal)
                    probs = jnp.exp2(scores * TO_LOG2 - stats[i, h, 0:1, columns])
                    low[n, h, 0, :, columns] = probs.astype(BF16)
                    dscores = probs * (dprobs - stats[i, h, 2:3, columns])
                    low[n, h, 1, :, columns] = dscores.astype(BF16)
            copy(n).start()
            return 0

        def add(n, _):
            e = lists[i, section, n]
            for h in range(HALF_KV):
                for w in range(2):
                    right = block[1 - w, h].reshape(ROWS, HEAD_DIM)
                    acc[e, 1 - w, h] += dot_nn(low[n, h, w], right)
            return 0

        def finish(n, _):
            copy(n).wait()
            return 0

        if first:
            look(0, True)
        lax.fori_loop(int(first), count, lambda n, _: look(n, False), 0)
        lax.fori_loop(0, count, add, 0)
        lax.fori_loop(0, count, finish, 0)
    write_grads(acc, outs)


def query_results(n_seq, lists, counts, place_ref, *rest):
    n_saved = 3
    n_pieces = n_seq // CORES
    saved, pieces, rest = rest[:n_saved], rest[n_saved:][: 2 * n_pieces], rest[n_saved + 2 * n_pieces :]
    table, *rest = rest
    outs, (store, low, out_acc, dq_acc, got) = rest[: 2 * HALF_KV], rest[2 * HALF_KV :]
    group, member, _ = here(n_seq)

    def copy(source, h, i, n, first):
        return pltpu.make_async_copy(source.at[i, n - first, h], low.at[h, i, n], got.at[h, i, n])

    ends = []
    for i in range(2):
        stops = [0]
        for section in range(n_saved):
            stops.append(stops[-1] + counts[i, section])
        ends.append(stops)
    for h in range(HALF_KV):
        for i, stops in enumerate(ends):
            for source, first, stop in zip(saved, stops, stops[1:]):

                def fetch_one(n, _):
                    copy(source, h, i, n, first).start()
                    return 0

                lax.fori_loop(first, stop, fetch_one, 0)
    fill(store, pieces)
    tables = []
    for i in range(2):
        mine = group * n_seq + lax.bitwise_xor(member, i)
        cosine, sine = block_tables(place_ref[mine], table)
        tables.append((cosine.T * SCALE, sine.T * SCALE))
    for h, (i, stops) in ((h, pair) for h in range(HALF_KV) for pair in enumerate(ends)):
        total = stops[-1]
        result = outs[i * HALF_KV + h]

        @pl.when(lax.rem(total, 2) == 1)
        def _():
            low[h, i, total] = jnp.zeros((2, BLK, ROWS), BF16)

        out_acc[...] = jnp.zeros_like(out_acc)
        dq_acc[...] = jnp.zeros_like(dq_acc)

        def add(n, _):
            pair = (2 * n, 2 * n + 1)
            for m in pair:
                for source, first, stop in zip(saved, stops, stops[1:]):

                    @pl.when(jnp.logical_and(m >= first, m < stop))
                    def _():
                        copy(source, h, i, m, first).wait()

            found = [lists[i, 3, m] for m in pair]
            keys_t = jnp.concatenate([store[e, 0, h].T for e in found], axis=1)
            values_t = jnp.concatenate([store[e, 1, h].T for e in found], axis=1)
            for _, columns in chunks():
                probs = jnp.concatenate([low[h, i, m, 0, :, columns] for m in pair], axis=0)
                dscores = jnp.concatenate([low[h, i, m, 1, :, columns] for m in pair], axis=0)
                out_acc[:, columns] += dot_nn(values_t, probs)
                dq_acc[:, columns] += dot_nn(keys_t, dscores)
            return 0

        lax.fori_loop(0, lax.div(total + 1, 2), add, 0)
        cosine, sine = tables[i]
        for r in range(RATIO):
            rows = slice(r * BLK, (r + 1) * BLK)
            columns = slice(r * HEAD_DIM, (r + 1) * HEAD_DIM)
            result[0, :, columns] = out_acc[:, rows].astype(BF16).T
            dq = dq_acc[:, rows]
            half = HEAD_DIM // 2
            turned = jnp.concatenate([dq[half:], dq[:half]], axis=0)
            result[1, :, columns] = (dq * cosine - turned * sine).astype(BF16).T


def finish_kv(n_seq, place_ref, *rest):
    *terms, table, keep, send = rest
    group, member, _ = here(n_seq)
    for i, result in enumerate((keep, send)):
        offset = lax.bitwise_xor(member, i)
        cosine, sine = block_tables(place_ref[group * n_seq + offset], table)
        for h in range(HALF_KV):
            columns = slice(h * HEAD_DIM, (h + 1) * HEAD_DIM)
            dk, dv = (sum(term[i, w, h].astype(F32) for term in terms) for w in range(2))
            result[0, :, columns] = turn(dk, cosine, -sine).astype(BF16)
            result[1, :, columns] = dv.astype(BF16)


def join_halves(*refs):
    core = lax.rem(lax.axis_index("seq"), CORES)
    own_q, got_q, (own_kv, got_kv) = refs[:HALF_KV], refs[HALF_KV:][:HALF_KV], refs[2 * HALF_KV :][:2]
    outs = refs[2 * HALF_KV + 2 :]
    for own, got, results in ((own_q, got_q, outs[:2]), ([own_kv], [got_kv], outs[2:])):
        width = own[0].shape[-1]
        for half, parts in ((core, own), (1 - core, got)):
            for n, part in enumerate(parts):
                start = pl.multiple_of((half * len(parts) + n) * width, width)
                for w, out in enumerate(results):
                    out[:, pl.ds(start, width)] = part[w]


def local(query_input, key_input, value_input, out_grad, key_blocks, key_counts, block_position):
    n_seq = lax.axis_size("seq")
    n_grp = lax.axis_size("grp")
    n_pieces = n_seq // CORES
    n_listed = key_blocks.shape[1]

    def cross(array, by):
        return lax.ppermute(array, "seq", [(m, m ^ by) for m in range(n_seq)])

    def along(array, by):
        return cross(array, CORES * by)

    def onward(array):
        return lax.ppermute(array, "grp", [(g, g + 1) for g in range(n_grp - 1)])

    def back(array):
        return lax.ppermute(array, "grp", [(g + 1, g) for g in range(n_grp - 1)])

    table = trig_table(block_position.shape[0])
    n_far = min(n_seq, n_listed - 1)
    split = 2 * CORES
    piece = (2, HALF_KV, BLK, HEAD_DIM)
    chip = (CORES, *piece)
    q_shape = jax.ShapeDtypeStruct((2, HALF_KV, RATIO, BLK, HEAD_DIM), BF16)
    kv_shape = jax.ShapeDtypeStruct(piece, BF16)
    stats_shape = jax.ShapeDtypeStruct((2, HALF_KV, 8, ROWS), F32)
    low = jax.ShapeDtypeStruct(chip, BF16)
    high = jax.ShapeDtypeStruct(chip, F32)
    lists, counts = call(
        functools.partial(make_lists, n_seq, split),
        (
            jax.ShapeDtypeStruct((2, 4, n_listed + 1), jnp.int32),
            jax.ShapeDtypeStruct((2, 4), jnp.int32),
        ),
        2, us=2, name="block_lists",
    )(key_blocks, key_counts)

    halves = pltpu.VMEM((CORES, query_input.shape[0], HEADS // CORES * HEAD_DIM), BF16)
    kv_keep, kv_send, q_keep, q_send = call(
        functools.partial(prepare, n_seq), (kv_shape, kv_shape, q_shape, q_shape), 1,
        [
            pltpu.VMEM(key_input.shape, BF16), pltpu.VMEM(value_input.shape, BF16),
            pltpu.VMEM(table.shape, F32), halves, halves, pltpu.VMEM(q_shape.shape, BF16),
            pltpu.SemaphoreType.DMA((8,)),
        ],
        us=3, name="prepare", n_hbm=5, hbm_out=2,
    )(block_position, key_input, value_input, query_input, out_grad, table)
    kv_got = cross(kv_send, 1)
    q_send, kv_got = lax.optimization_barrier((q_send, kv_got))
    q_got = cross(q_send, 1)
    near = [jnp.stack([kv_keep, kv_got])]
    near.append(along(near[0], 1))
    ready, first_far = lax.optimization_barrier((near[1], onward(near[0])))
    far = [first_far, None]
    for k in range(2, n_pieces, 2):
        piece_k, lists, counts, _ = lax.optimization_barrier(
            (along(near[0], k), lists, counts, ready)
        )
        near += [piece_k, along(piece_k, 1)]
        far += [onward(piece_k), None]
    stats = call(
        functools.partial(current_stats, 1), stats_shape, 2, [pltpu.VMEM((split, *piece), BF16)],
        us=4, name="near_statistics", hold=(2,),
    )(lists, counts, q_keep, q_got, *near[:2])
    ready, far[2], stats = lax.optimization_barrier((ready, far[2], stats))
    far[1] = onward(ready)
    for k in range(2, n_pieces, 2):
        far[k + 1] = along(far[k], 1)
    stats = call(
        functools.partial(current_stats, 2), stats_shape, 2,
        [pltpu.VMEM((n_seq - split, *piece), BF16)], us=4, name="far_statistics",
    )(lists, counts, q_keep, q_got, stats, *near[2:])

    def grads_call(kernel, n_slots, n_store, outs, us, name, kept=(), more=()):
        pair = (n_slots, HALF_KV, 2, BLK, ROWS)
        saved = jax.ShapeDtypeStruct((2, *pair), BF16)
        return call(
            kernel, (*outs, saved, *more), 2,
            [
                pltpu.VMEM((n_store, *piece), BF16), pltpu.VMEM((n_store, *piece), F32),
                pltpu.VMEM(pair, BF16), pltpu.SemaphoreType.DMA((n_slots,)), *kept,
            ],
            us=us, name=name, hbm_out=len(outs),
        )

    kept = pltpu.VMEM((n_far, HALF_KV, BLK, ROWS), F32)
    two = jax.ShapeDtypeStruct((2 * CORES, *piece), BF16)
    first_far, *far_grads, far_saved, stats = grads_call(
        functools.partial(previous_grads, n_pieces), n_far, n_seq, (two,) + (low,) * (n_pieces - 2),
        14, "previous_gradients", (kept, kept), (stats_shape,),
    )(lists, counts, q_keep, q_got, stats, *far)

    def current_call(section, outs, name, pieces, after):
        stats_late, _ = lax.optimization_barrier((stats, after))
        n_store = CORES * len(pieces)
        *grads, saved = grads_call(
            functools.partial(current_grads, section, len(pieces)), min(n_store, n_listed), n_store,
            outs, 6, name,
        )(lists, counts, q_keep, q_got, stats_late, *pieces)
        return grads, saved

    def total(*terms):
        return sum(term.astype(F32) for term in terms).astype(BF16)

    from_far = back(first_far)
    crossing = [along(grad, 1) for grad in far_grads[1::2]]
    high_grads, high_saved = current_call(
        2, [high, low] * (n_pieces // 2 - 1), "far_current_gradients", near[2:], far_grads[0]
    )
    crossing, high_grads = lax.optimization_barrier((crossing, high_grads))
    arrived = [
        back(total(grad, extra)) for grad, extra in zip(far_grads[0::2], crossing)
    ]
    swapped = [along(grad, 1) for grad in high_grads[1::2]]
    low_grads, low_saved = current_call(
        1, [high, high], "near_current_gradients", near[:2], high_grads[0]
    )
    low_grads, from_far = lax.optimization_barrier((low_grads, from_far))
    from_next = along(total(low_grads[1], from_far[CORES:]), 1)
    merged = [
        total(*terms) for terms in zip(high_grads[0::2], arrived, swapped)
    ]
    half_out = jax.ShapeDtypeStruct((2, BLK, RATIO * HEAD_DIM), BF16)
    place_late, _ = lax.optimization_barrier((block_position, merged))
    wide = pltpu.VMEM((HEAD_DIM, ROWS), F32)
    slots = (HALF_KV, 2, n_listed + 1)
    halves = call(
        functools.partial(query_results, n_seq), (half_out,) * (2 * HALF_KV), 3,
        [
            pltpu.VMEM((2 * n_seq, *piece), BF16), pltpu.VMEM((*slots, 2, BLK, ROWS), BF16),
            wide, wide, pltpu.SemaphoreType.DMA(slots),
        ],
        us=20, name="query_results", n_hbm=3,
    )(lists, counts, place_late, far_saved, low_saved, high_saved, *far, *near, table)
    own_halves, other_halves = halves[:HALF_KV], halves[HALF_KV:]
    other_halves = lax.optimization_barrier(list(other_halves))
    got_halves = [cross(half, 1) for half in other_halves]
    final = [low_grads[0], from_far[:CORES], from_next]
    final += [along(part, 2 + 2 * n) for n, part in enumerate(merged)]
    own_halves = list(own_halves)
    final[0], own_halves[1] = lax.optimization_barrier((final[0], own_halves[1]))
    kv_half = jax.ShapeDtypeStruct((2, BLK, HALF_KV * HEAD_DIM), BF16)
    own_kv, other_kv = call(
        functools.partial(finish_kv, n_seq), (kv_half, kv_half), 1, us=2, name="key_gradients"
    )(block_position, *final, table)
    got_kv = cross(other_kv, 1)
    q_out = jax.ShapeDtypeStruct(query_input.shape, BF16)
    kv_out = jax.ShapeDtypeStruct(key_input.shape, BF16)
    out_rows, query_grad, key_grad, value_grad = call(
        join_halves, (q_out, q_out, kv_out, kv_out), 0, us=2, name="join_halves"
    )(*own_halves, *got_halves, own_kv, got_kv)
    return (out_rows, query_grad, key_grad, value_grad)


def solution(mesh):
    split = P(("grp", "seq"), None)
    return jax.shard_map(
        local,
        mesh=mesh,
        in_specs=(split, split, split, split, P(), P(), P()),
        out_specs=(split, split, split, split),
        check_vma=False,
    )
```

profile of v0, /device:TPU:5, one launch (start us, length us, event | category | flops | bytes accessed | tf_op | source)
XLA Modules:
  0.0 96.2 jit_solution(2456899012879052338)
XLA Ops:
  0.6 0.0 copy-start.4
  0.6 3.5 %prepare.1 = (bf16[2,2,128,128]{3,2,1,0:T(8,128)(2,1)S(1)}, bf16[2,2,128,128]{3,2,1,0:T(8,128)(2,1)S(1)}, bf16[2,2,8,128,128]{4,3,2,1,0:T(8,128)(2,1)}, bf16[2,2,8,128,128]{4,3,2,1,0:T(8,128)(2,1)S(1)}) custom-call(s32[32]{0:T(128)} %place_ref.4, bf16[128,512]{1,0:T(8,128)(2,1)} %refs_0_.1, bf16[128,512]{1,0:T(8,128)(2,1)} %refs_1_.1, ...), custom_call_target="tpu_custom_call" | custom-call | flops 3000000000 | bytes 1048576 | tf_op jit(solution)/shard_map/prepare/pallas_call | solution.py:99
  4.2 0.7 collective-permute-start
  4.9 1.0 %collective-permute-done = bf16[2,2,128,128]{3,2,1,0:T(8,128)(2,1)S(1)} collective-permute-done((bf16[2,2,128,128]{3,2,1,0:T(8,128)(2,1)S(1)}, bf16[2,2,128,128]{3,2,1,0:T(8,128)(2,1)S(1)}, u32[]{:S(2)}, u32[]{:S(2)}) %collective-permute-start) | collective-permute-done | bytes 131104 | tf_op jit(solution)/shard_map/ppermute | solution.py:507
  5.9 0.4 collective-permute-start.4
  6.3 3.1 %collective-permute-start.3 = (bf16[2,2,2,128,128]{4,3,2,1,0:T(8,128)(2,1)S(1)}, bf16[2,2,2,128,128]{4,3,2,1,0:T(8,128)(2,1)S(1)}, u32[]{:S(2)}, u32[]{:S(2)}) collective-permute-start(bf16[2,2,2,128,128]{4,3,2,1,0:T(8,128)(2,1)S(1)} %pad_maximum_fusion.rest_0_.rest_7_), channel_id=1, source_target_pairs={{0,8},{8,16},{16,24},{1,9},{9,17},{17,25},{2,10},{10,18},{18,26},{... | collective-permute-start | bytes 786440 | tf_op jit(solution)/shard_map/ppermute | solution.py:513
  9.4 1.4 %collective-permute-start.2 = (bf16[2,2,2,128,128]{4,3,2,1,0:T(8,128)(2,1)S(1)}, bf16[2,2,2,128,128]{4,3,2,1,0:T(8,128)(2,1)S(1)}, u32[]{:S(2)}, u32[]{:S(2)}) collective-permute-start(bf16[2,2,2,128,128]{4,3,2,1,0:T(8,128)(2,1)S(1)} %pad_maximum_fusion.rest_0_.rest_7_), channel_id=1, source_target_pairs={{0,2},{1,3},{2,0},{3,1},{4,6},{5,7},{6,4},{7,5},{8,10},{9,11},{10,... | collective-permute-start | bytes 786440 | tf_op jit(solution)/shard_map/ppermute | solution.py:507
  10.8 2.3 %collective-permute-start.1 = (bf16[2,2,2,128,128]{4,3,2,1,0:T(8,128)(2,1)S(1)}, bf16[2,2,2,128,128]{4,3,2,1,0:T(8,128)(2,1)S(1)}, u32[]{:S(2)}, u32[]{:S(2)}) collective-permute-start(bf16[2,2,2,128,128]{4,3,2,1,0:T(8,128)(2,1)S(1)} %pad_maximum_fusion.rest_0_.rest_7_), channel_id=1, source_target_pairs={{0,4},{1,5},{2,6},{3,7},{4,0},{5,1},{6,2},{7,3},{8,12},{9,13},{10,... | collective-permute-start | bytes 786440 | tf_op jit(solution)/shard_map/ppermute | solution.py:507
  13.1 0.0 copy-done.4
  13.1 0.7 copy.12.key_blocks
  13.8 1.9 %block_lists.1 = (s32[2,4,13]{2,1,0:T(4,128)S(1)}, s32[2,4]{1,0:T(2,128)S(1)}) custom-call(s32[32,12]{1,0:T(8,128)} %copy.12.key_blocks, s32[32]{0:T(128)} %key_counts.1), custom_call_target="tpu_custom_call" | custom-call | flops 2000000000 | bytes 1048576 | tf_op jit(solution)/shard_map/block_lists/pallas_call | solution.py:99
  15.7 0.0 copy-start.2
  15.7 0.6 copy-done.2
  16.3 0.0 copy-start.3
  16.3 0.0 copy-start.1
  16.3 0.5 collective-permute-done.3.rest_0_.rest_3_
  16.9 5.6 %collective-permute-done.2.rest_1_.rest_8_ = bf16[2,2,2,128,128]{4,3,2,1,0:T(8,128)(2,1)S(1)} collective-permute-done((bf16[2,2,2,128,128]{4,3,2,1,0:T(8,128)(2,1)S(1)}, bf16[2,2,2,128,128]{4,3,2,1,0:T(8,128)(2,1)S(1)}, u32[]{:S(2)}, u32[]{:S(2)}) %collective-permute-start.2) | collective-permute-done | bytes 262176 | tf_op jit(solution)/shard_map/ppermute | solution.py:507
  22.4 0.0 collective-permute-done.1.rest_1_.rest_0_.rest_9_
  22.5 2.5 %collective-permute-start.6 = (bf16[2,2,2,128,128]{4,3,2,1,0:T(8,128)(2,1)S(1)}, bf16[2,2,2,128,128]{4,3,2,1,0:T(8,128)(2,1)S(1)}, u32[]{:S(2)}, u32[]{:S(2)}) collective-permute-start(bf16[2,2,2,128,128]{4,3,2,1,0:T(8,128)(2,1)S(1)} %collective-permute-done.1.rest_1_.rest_0_.rest_9_), channel_id=1, source_target_pairs={{0,2},{1,3},{2,0},{3,1},{4,6},{5,7},{6,4},{7,5},{8,10},{9,11},{10,... | collective-permute-start | bytes 786440 | tf_op jit(solution)/shard_map/ppermute | solution.py:507
  24.9 1.9 %collective-permute-start.5 = (bf16[2,2,2,128,128]{4,3,2,1,0:T(8,128)(2,1)S(1)}, bf16[2,2,2,128,128]{4,3,2,1,0:T(8,128)(2,1)S(1)}, u32[]{:S(2)}, u32[]{:S(2)}) collective-permute-start(bf16[2,2,2,128,128]{4,3,2,1,0:T(8,128)(2,1)S(1)} %collective-permute-done.1.rest_1_.rest_0_.rest_9_), channel_id=1, source_target_pairs={{0,8},{8,16},{16,24},{1,9},{9,17},{17,25},{2,10},{10,18},{18,26},{... | collective-permute-start | bytes 786440 | tf_op jit(solution)/shard_map/ppermute | solution.py:513
  26.8 0.0 collective-permute-done.4.other
  26.8 0.0 copy-done.3
  26.9 2.4 %near_statistics.1.rest_0_ = f32[2,2,8,1024]{3,2,1,0:T(8,128)S(1)} custom-call(s32[2,4,13]{2,1,0:T(4,128)} %copy-done.2, s32[2,4]{1,0:T(2,128)} %copy-done.3, bf16[2,2,8,128,128]{4,3,2,1,0:T(8,128)(2,1)} %get-tuple-element.59.own, bf16[2,2,8,128,128]{4,3,2,1,0:T(8,128)(2,1)S(1)} %collective-permute-done.4.other, ...), custom_call_target="tpu_custom_call" | custom-call | flops 4000000000 | bytes 1048576 | tf_op jit(solution)/shard_map/near_statistics/pallas_call | solution.py:99
  29.2 4.7 %collective-permute-done.5.rest_2_.rest_5_ = bf16[2,2,2,128,128]{4,3,2,1,0:T(8,128)(2,1)S(1)} collective-permute-done((bf16[2,2,2,128,128]{4,3,2,1,0:T(8,128)(2,1)S(1)}, bf16[2,2,2,128,128]{4,3,2,1,0:T(8,128)(2,1)S(1)}, u32[]{:S(2)}, u32[]{:S(2)}) %collective-permute-start.5) | collective-permute-done | bytes 262176 | tf_op jit(solution)/shard_map/ppermute | solution.py:513
  33.9 1.9 %collective-permute-start.7 = (bf16[2,2,2,128,128]{4,3,2,1,0:T(8,128)(2,1)S(1)}, bf16[2,2,2,128,128]{4,3,2,1,0:T(8,128)(2,1)S(1)}, u32[]{:S(2)}, u32[]{:S(2)}) collective-permute-start(bf16[2,2,2,128,128]{4,3,2,1,0:T(8,128)(2,1)S(1)} %collective-permute-done.2.rest_1_.rest_8_), channel_id=1, source_target_pairs={{0,8},{8,16},{16,24},{1,9},{9,17},{17,25},{2,10},{10,18},{18,26},{... | collective-permute-start | bytes 786440 | tf_op jit(solution)/shard_map/ppermute | solution.py:513
  35.8 0.1 collective-permute-start.8
  35.9 0.0 collective-permute-done.6.rest_2_.rest_1_.rest_10_
  35.9 0.0 copy-done.1
  35.9 0.8 far_statistics.1.stats_in
  36.7 5.2 %collective-permute-done.7.rest_1_.rest_4_ = bf16[2,2,2,128,128]{4,3,2,1,0:T(8,128)(2,1)S(1)} collective-permute-done((bf16[2,2,2,128,128]{4,3,2,1,0:T(8,128)(2,1)S(1)}, bf16[2,2,2,128,128]{4,3,2,1,0:T(8,128)(2,1)S(1)}, u32[]{:S(2)}, u32[]{:S(2)}) %collective-permute-start.7) | collective-permute-done | bytes 262176 | tf_op jit(solution)/shard_map/ppermute | solution.py:513
  41.9 0.0 collective-permute-done.8.rest_3_.rest_6_
  41.9 11.7 %previous_gradients.1 = (bf16[4,2,2,128,128]{4,3,2,1,0:T(8,128)(2,1)S(1)}, bf16[2,2,2,128,128]{4,3,2,1,0:T(8,128)(2,1)S(1)}, bf16[2,2,2,128,128]{4,3,2,1,0:T(8,1...) custom-call(s32[2,4,13]{2,1,0:T(4,128)} %copy-done.2, s32[2,4]{1,0:T(2,128)} %copy-done.3, ...), custom_call_target="tpu_custom_call" | custom-call | flops 14000000000 | bytes 1048576 | tf_op jit(solution)/shard_map/previous_gradients/pallas_call | solution.py:99
  53.6 1.3 %collective-permute-start.9 = (bf16[2,2,2,128,128]{4,3,2,1,0:T(8,128)(2,1)S(1)}, bf16[2,2,2,128,128]{4,3,2,1,0:T(8,128)(2,1)S(1)}, u32[]{:S(2)}, u32[]{:S(2)}) collective-permute-start(bf16[2,2,2,128,128]{4,3,2,1,0:T(8,128)(2,1)S(1)} %get-tuple-element.66), channel_id=1, source_target_pairs={{0,2},{1,3},{2,0},{3,1},{4,6},{5,7},{6,4},{7,5},{8,10},{9,11},{10,... | collective-permute-start | bytes 786440 | tf_op jit(solution)/shard_map/ppermute | solution.py:507
  54.8 5.5 %collective-permute-start.12 = (bf16[4,2,2,128,128]{4,3,2,1,0:T(8,128)(2,1)S(1)}, bf16[4,2,2,128,128]{4,3,2,1,0:T(8,128)(2,1)S(1)}, u32[]{:S(2)}, u32[]{:S(2)}) collective-permute-start(bf16[4,2,2,128,128]{4,3,2,1,0:T(8,128)(2,1)S(1)} %get-tuple-element.83), channel_id=1, source_target_pairs={{8,0},{16,8},{24,16},{9,1},{17,9},{25,17},{10,2},{18,10},{26,18},{... | collective-permute-start | bytes 1572872 | tf_op jit(solution)/shard_map/ppermute | solution.py:516
  60.3 1.0 %far_current_gradients.1 = (f32[2,2,2,128,128]{4,3,2,1,0:T(8,128)S(1)}, bf16[2,2,2,128,128]{4,3,2,1,0:T(8,128)(2,1)S(1)}, bf16[2,4,2,2,128,1024]{5,4,3,2,1,0:T(8,128)(2,1)}) custom-call(s32[2,4,13]{2,1,0:T(4,128)} %copy-done.2, s32[2,4]{1,0:T(2,128)} %copy-done.3, bf16[2,2,8,128,128]{4,3,2,1,0:T(8,128)(2,1)S(1)} %copy-done.1, ...), custom_call_target="tpu_custom_call" | custom-call | flops 6000000000 | bytes 1048576 | tf_op jit(solution)/shard_map/far_current_gradients/pallas_call | solution.py:99
  61.3 0.0 collective-permute-done.9
  61.3 0.1 add_convert_fusion.2
  61.4 0.0 copy-start
  61.4 4.3 %collective-permute-start.10 = (bf16[2,2,2,128,128]{4,3,2,1,0:T(8,128)(2,1)S(1)}, bf16[2,2,2,128,128]{4,3,2,1,0:T(8,128)(2,1)S(1)}, u32[]{:S(2)}, u32[]{:S(2)}) collective-permute-start(bf16[2,2,2,128,128]{4,3,2,1,0:T(8,128)(2,1)S(1)} %add_convert_fusion.2), channel_id=1, source_target_pairs={{8,0},{16,8},{24,16},{9,1},{17,9},{25,17},{10,2},{18,10},{26,18},{... | collective-permute-start | bytes 786440 | tf_op jit(solution)/shard_map/ppermute | solution.py:516
  65.8 0.1 collective-permute-start.11
  65.8 3.8 %near_current_gradients.1 = (f32[2,2,2,128,128]{4,3,2,1,0:T(8,128)S(1)}, f32[2,2,2,128,128]{4,3,2,1,0:T(8,128)S(1)}, bf16[2,4,2,2,128,1024]{5,4,3,2,1,0:T(8,128)(2,1)}) custom-call(s32[2,4,13]{2,1,0:T(4,128)} %copy-done.2, s32[2,4]{1,0:T(2,128)} %copy-done.3, bf16[2,2,8,128,128]{4,3,2,1,0:T(8,128)(2,1)S(1)} %copy-done.1, ...), custom_call_target="tpu_custom_call" | custom-call | flops 6000000000 | bytes 1048576 | tf_op jit(solution)/shard_map/near_current_gradients/pallas_call | solution.py:99
  69.7 3.7 %collective-permute-done.10 = bf16[2,2,2,128,128]{4,3,2,1,0:T(8,128)(2,1)S(1)} collective-permute-done((bf16[2,2,2,128,128]{4,3,2,1,0:T(8,128)(2,1)S(1)}, bf16[2,2,2,128,128]{4,3,2,1,0:T(8,128)(2,1)S(1)}, u32[]{:S(2)}, u32[]{:S(2)}) %collective-permute-start.10) | collective-permute-done | bytes 262176 | tf_op jit(solution)/shard_map/ppermute | solution.py:516
  73.4 0.0 collective-permute-done.11
  73.4 0.1 add_convert_fusion.1
  73.5 4.9 %collective-permute-start.16 = (bf16[2,2,2,128,128]{4,3,2,1,0:T(8,128)(2,1)S(1)}, bf16[2,2,2,128,128]{4,3,2,1,0:T(8,128)(2,1)S(1)}, u32[]{:S(2)}, u32[]{:S(2)}) collective-permute-start(bf16[2,2,2,128,128]{4,3,2,1,0:T(8,128)(2,1)S(1)} %add_convert_fusion.1), channel_id=1, source_target_pairs={{0,4},{1,5},{2,6},{3,7},{4,0},{5,1},{6,2},{7,3},{8,12},{9,13},{10,... | collective-permute-start | bytes 786440 | tf_op jit(solution)/shard_map/ppermute | solution.py:507
  78.4 0.0 collective-permute-done.12
  78.4 0.1 add_convert_fusion
  78.5 0.1 collective-permute-start.15
  78.5 0.0 copy-done
  78.5 7.9 %query_results.1 = (bf16[2,128,1024]{2,1,0:T(8,128)(2,1)S(1)}, bf16[2,128,1024]{2,1,0:T(8,128)(2,1)S(1)}, bf16[2,128,1024]{2,1,0:T(8,128)(2,1)S(1)}, bf16[2,128,1024]{2,1,0:T(8,128)(2,1)S(1)}) custom-call(s32[2,4,13]{2,1,0:T(4,128)} %copy-done.2, s32[2,4]{1,0:T(2,128)} %copy-done.3, s32[32]{0:T(128)} %place_ref.4, ...), custom_call_target="tpu_custom_call" | custom-call | flops 20000000000 | bytes 1048576 | tf_op jit(solution)/shard_map/query_results/pallas_call | solution.py:99
  86.5 5.1 %collective-permute-start.13 = (bf16[2,128,1024]{2,1,0:T(8,128)(2,1)S(1)}, bf16[2,128,1024]{2,1,0:T(8,128)(2,1)S(1)}, u32[]{:S(2)}, u32[]{:S(2)}) collective-permute-start(bf16[2,128,1024]{2,1,0:T(8,128)(2,1)S(1)} %get-tuple-element.89), channel_id=1, source_target_pairs={{0,1},{1,0},{2,3},{3,2},{4,5},{5,4},{6,7},{7,6},{8,9},{9,8},{10,11... | collective-permute-start | bytes 1572872 | tf_op jit(solution)/shard_map/ppermute | solution.py:507
  91.6 0.1 collective-permute-start.14
  91.7 0.0 collective-permute-done.16.rest_3_
  91.7 0.0 collective-permute-done.15.rest_2_
  91.7 0.9 key_gradients.1
  92.6 1.1 %collective-permute-start.17 = (bf16[2,128,256]{2,1,0:T(8,128)(2,1)S(1)}, bf16[2,128,256]{2,1,0:T(8,128)(2,1)S(1)}, u32[]{:S(2)}, u32[]{:S(2)}) collective-permute-start(bf16[2,128,256]{2,1,0:T(8,128)(2,1)S(1)} %get-tuple-element.95), channel_id=1, source_target_pairs={{0,1},{1,0},{2,3},{3,2},{4,5},{5,4},{6,7},{7,6},{8,9},{9,8},{10,11... | collective-permute-start | bytes 393224 | tf_op jit(solution)/shard_map/ppermute | solution.py:507
  93.7 1.0 %collective-permute-done.17.refs_5_ = bf16[2,128,256]{2,1,0:T(8,128)(2,1)S(1)} collective-permute-done((bf16[2,128,256]{2,1,0:T(8,128)(2,1)S(1)}, bf16[2,128,256]{2,1,0:T(8,128)(2,1)S(1)}, u32[]{:S(2)}, u32[]{:S(2)}) %collective-permute-start.17) | collective-permute-done | bytes 131104 | tf_op jit(solution)/shard_map/ppermute | solution.py:507
  94.7 0.0 collective-permute-done.13.refs_2_
  94.7 0.0 collective-permute-done.14.refs_3_
  94.7 1.6 %join_halves.1 = (bf16[128,4096]{1,0:T(8,128)(2,1)}, bf16[128,4096]{1,0:T(8,128)(2,1)}, bf16[128,512]{1,0:T(8,128)(2,1)}, bf16[128,512]{1,0:T(8,128)(2,1)}) custom-call(bf16[2,128,1024]{2,1,0:T(8,128)(2,1)S(1)} %get-tuple-element.80.refs_0_, bf16[2,128,1024]{2,1,0:T(8,128)(2,1)S(1)} %get-tuple-element.86.refs_1_, ...), custom_call_target="tpu_custom_call" | custom-call | flops 2000000000 | bytes 1048576 | tf_op jit(solution)/shard_map/join_halves/pallas_call | solution.py:99
  (2 shorter events, 0.0 us)
Async XLA Ops:
  0.6 12.5 %copy-start.4 = (s32[32,12]{0,1:T(8,128)S(1)}, s32[32,12]{0,1:T(8,128)}, u32[]{:S(2)}) copy-start(s32[32,12]{0,1:T(8,128)} %param.12) | copy-start | bytes 4612
  4.2 1.7 %collective-permute-start = (bf16[2,2,128,128]{3,2,1,0:T(8,128)(2,1)S(1)}, bf16[2,2,128,128]{3,2,1,0:T(8,128)(2,1)S(1)}, u32[]{:S(2)}, u32[]{:S(2)}) collective-permute-start(bf16[2,2,128,128]{3,2,1,0:T(8,128)(2,1)S(1)} %get-tuple-element.52), channel_id=1, source_target_pairs={{0,1},{1,0},{2,3},{3,2},{4,5},{5,4},{6,7},{7,6},{8,9},{9,8},{10,11... | collective-permute-start | bytes 393224 | tf_op jit(solution)/shard_map/ppermute | solution.py:507
  5.9 20.9 %collective-permute-start.4 = (bf16[2,2,8,128,128]{4,3,2,1,0:T(8,128)(2,1)S(1)}, bf16[2,2,8,128,128]{4,3,2,1,0:T(8,128)(2,1)S(1)}, u32[]{:S(2)}, u32[]{:S(2)}) collective-permute-start(bf16[2,2,8,128,128]{4,3,2,1,0:T(8,128)(2,1)S(1)} %get-tuple-element.60), channel_id=1, source_target_pairs={{0,1},{1,0},{2,3},{3,2},{4,5},{5,4},{6,7},{7,6},{8,9},{9,8},{10,11... | collective-permute-start | bytes 3145736 | tf_op jit(solution)/shard_map/ppermute | solution.py:507
  6.3 10.5 %collective-permute-start.3 = (bf16[2,2,2,128,128]{4,3,2,1,0:T(8,128)(2,1)S(1)}, bf16[2,2,2,128,128]{4,3,2,1,0:T(8,128)(2,1)S(1)}, u32[]{:S(2)}, u32[]{:S(2)}) collective-permute-start(bf16[2,2,2,128,128]{4,3,2,1,0:T(8,128)(2,1)S(1)} %pad_maximum_fusion.rest_0_.rest_7_), channel_id=1, source_target_pairs={{0,8},{8,16},{16,24},{1,9},{9,17},{17,25},{2,10},{10,18},{18,26},{... | collective-permute-start | bytes 786440 | tf_op jit(solution)/shard_map/ppermute | solution.py:513
  9.4 13.0 %collective-permute-start.2 = (bf16[2,2,2,128,128]{4,3,2,1,0:T(8,128)(2,1)S(1)}, bf16[2,2,2,128,128]{4,3,2,1,0:T(8,128)(2,1)S(1)}, u32[]{:S(2)}, u32[]{:S(2)}) collective-permute-start(bf16[2,2,2,128,128]{4,3,2,1,0:T(8,128)(2,1)S(1)} %pad_maximum_fusion.rest_0_.rest_7_), channel_id=1, source_target_pairs={{0,2},{1,3},{2,0},{3,1},{4,6},{5,7},{6,4},{7,5},{8,10},{9,11},{10,... | collective-permute-start | bytes 786440 | tf_op jit(solution)/shard_map/ppermute | solution.py:507
  10.8 11.6 %collective-permute-start.1 = (bf16[2,2,2,128,128]{4,3,2,1,0:T(8,128)(2,1)S(1)}, bf16[2,2,2,128,128]{4,3,2,1,0:T(8,128)(2,1)S(1)}, u32[]{:S(2)}, u32[]{:S(2)}) collective-permute-start(bf16[2,2,2,128,128]{4,3,2,1,0:T(8,128)(2,1)S(1)} %pad_maximum_fusion.rest_0_.rest_7_), channel_id=1, source_target_pairs={{0,4},{1,5},{2,6},{3,7},{4,0},{5,1},{6,2},{7,3},{8,12},{9,13},{10,... | collective-permute-start | bytes 786440 | tf_op jit(solution)/shard_map/ppermute | solution.py:507
  15.7 0.6 copy-start.2
  16.3 10.5 %copy-start.3 = (s32[2,4]{1,0:T(2,128)}, s32[2,4]{1,0:T(2,128)S(1)}, u32[]{:S(2)}) copy-start(s32[2,4]{1,0:T(2,128)S(1)} %get-tuple-element.58.counts) | copy-start | bytes 100
  16.3 19.6 %copy-start.1 = (bf16[2,2,8,128,128]{4,3,2,1,0:T(8,128)(2,1)S(1)}, bf16[2,2,8,128,128]{4,3,2,1,0:T(8,128)(2,1)}, u32[]{:S(2)}) copy-start(bf16[2,2,8,128,128]{4,3,2,1,0:T(8,128)(2,1)} %get-tuple-element.59.own) | copy-start | bytes 3145732
  22.5 13.4 %collective-permute-start.6 = (bf16[2,2,2,128,128]{4,3,2,1,0:T(8,128)(2,1)S(1)}, bf16[2,2,2,128,128]{4,3,2,1,0:T(8,128)(2,1)S(1)}, u32[]{:S(2)}, u32[]{:S(2)}) collective-permute-start(bf16[2,2,2,128,128]{4,3,2,1,0:T(8,128)(2,1)S(1)} %collective-permute-done.1.rest_1_.rest_0_.rest_9_), channel_id=1, source_target_pairs={{0,2},{1,3},{2,0},{3,1},{4,6},{5,7},{6,4},{7,5},{8,10},{9,11},{10,... | collective-permute-start | bytes 786440 | tf_op jit(solution)/shard_map/ppermute | solution.py:507
  24.9 9.0 %collective-permute-start.5 = (bf16[2,2,2,128,128]{4,3,2,1,0:T(8,128)(2,1)S(1)}, bf16[2,2,2,128,128]{4,3,2,1,0:T(8,128)(2,1)S(1)}, u32[]{:S(2)}, u32[]{:S(2)}) collective-permute-start(bf16[2,2,2,128,128]{4,3,2,1,0:T(8,128)(2,1)S(1)} %collective-permute-done.1.rest_1_.rest_0_.rest_9_), channel_id=1, source_target_pairs={{0,8},{8,16},{16,24},{1,9},{9,17},{17,25},{2,10},{10,18},{18,26},{... | collective-permute-start | bytes 786440 | tf_op jit(solution)/shard_map/ppermute | solution.py:513
  33.9 8.0 %collective-permute-start.7 = (bf16[2,2,2,128,128]{4,3,2,1,0:T(8,128)(2,1)S(1)}, bf16[2,2,2,128,128]{4,3,2,1,0:T(8,128)(2,1)S(1)}, u32[]{:S(2)}, u32[]{:S(2)}) collective-permute-start(bf16[2,2,2,128,128]{4,3,2,1,0:T(8,128)(2,1)S(1)} %collective-permute-done.2.rest_1_.rest_8_), channel_id=1, source_target_pairs={{0,8},{8,16},{16,24},{1,9},{9,17},{17,25},{2,10},{10,18},{18,26},{... | collective-permute-start | bytes 786440 | tf_op jit(solution)/shard_map/ppermute | solution.py:513
  35.8 6.1 %collective-permute-start.8 = (bf16[2,2,2,128,128]{4,3,2,1,0:T(8,128)(2,1)S(1)}, bf16[2,2,2,128,128]{4,3,2,1,0:T(8,128)(2,1)S(1)}, u32[]{:S(2)}, u32[]{:S(2)}) collective-permute-start(bf16[2,2,2,128,128]{4,3,2,1,0:T(8,128)(2,1)S(1)} %collective-permute-done.5.rest_2_.rest_5_), channel_id=1, source_target_pairs={{0,2},{1,3},{2,0},{3,1},{4,6},{5,7},{6,4},{7,5},{8,10},{9,11},{10,... | collective-permute-start | bytes 786440 | tf_op jit(solution)/shard_map/ppermute | solution.py:507
  53.6 7.8 %collective-permute-start.9 = (bf16[2,2,2,128,128]{4,3,2,1,0:T(8,128)(2,1)S(1)}, bf16[2,2,2,128,128]{4,3,2,1,0:T(8,128)(2,1)S(1)}, u32[]{:S(2)}, u32[]{:S(2)}) collective-permute-start(bf16[2,2,2,128,128]{4,3,2,1,0:T(8,128)(2,1)S(1)} %get-tuple-element.66), channel_id=1, source_target_pairs={{0,2},{1,3},{2,0},{3,1},{4,6},{5,7},{6,4},{7,5},{8,10},{9,11},{10,... | collective-permute-start | bytes 786440 | tf_op jit(solution)/shard_map/ppermute | solution.py:507
  54.8 23.6 %collective-permute-start.12 = (bf16[4,2,2,128,128]{4,3,2,1,0:T(8,128)(2,1)S(1)}, bf16[4,2,2,128,128]{4,3,2,1,0:T(8,128)(2,1)S(1)}, u32[]{:S(2)}, u32[]{:S(2)}) collective-permute-start(bf16[4,2,2,128,128]{4,3,2,1,0:T(8,128)(2,1)S(1)} %get-tuple-element.83), channel_id=1, source_target_pairs={{8,0},{16,8},{24,16},{9,1},{17,9},{25,17},{10,2},{18,10},{26,18},{... | collective-permute-start | bytes 1572872 | tf_op jit(solution)/shard_map/ppermute | solution.py:516
  61.4 17.1 %copy-start = (f32[320,128]{1,0:T(8,128)S(1)}, f32[320,128]{1,0:T(8,128)}, u32[]{:S(2)}) copy-start(f32[320,128]{1,0:T(8,128)} %constant.2.clone.refs_4_.rest_11_.rest_4_) | copy-start | bytes 491524
  61.4 12.0 %collective-permute-start.10 = (bf16[2,2,2,128,128]{4,3,2,1,0:T(8,128)(2,1)S(1)}, bf16[2,2,2,128,128]{4,3,2,1,0:T(8,128)(2,1)S(1)}, u32[]{:S(2)}, u32[]{:S(2)}) collective-permute-start(bf16[2,2,2,128,128]{4,3,2,1,0:T(8,128)(2,1)S(1)} %add_convert_fusion.2), channel_id=1, source_target_pairs={{8,0},{16,8},{24,16},{9,1},{17,9},{25,17},{10,2},{18,10},{26,18},{... | collective-permute-start | bytes 786440 | tf_op jit(solution)/shard_map/ppermute | solution.py:516
  65.8 7.7 %collective-permute-start.11 = (bf16[2,2,2,128,128]{4,3,2,1,0:T(8,128)(2,1)S(1)}, bf16[2,2,2,128,128]{4,3,2,1,0:T(8,128)(2,1)S(1)}, u32[]{:S(2)}, u32[]{:S(2)}) collective-permute-start(bf16[2,2,2,128,128]{4,3,2,1,0:T(8,128)(2,1)S(1)} %get-tuple-element.74), channel_id=1, source_target_pairs={{0,2},{1,3},{2,0},{3,1},{4,6},{5,7},{6,4},{7,5},{8,10},{9,11},{10,... | collective-permute-start | bytes 786440 | tf_op jit(solution)/shard_map/ppermute | solution.py:507
  73.5 18.2 %collective-permute-start.16 = (bf16[2,2,2,128,128]{4,3,2,1,0:T(8,128)(2,1)S(1)}, bf16[2,2,2,128,128]{4,3,2,1,0:T(8,128)(2,1)S(1)}, u32[]{:S(2)}, u32[]{:S(2)}) collective-permute-start(bf16[2,2,2,128,128]{4,3,2,1,0:T(8,128)(2,1)S(1)} %add_convert_fusion.1), channel_id=1, source_target_pairs={{0,4},{1,5},{2,6},{3,7},{4,0},{5,1},{6,2},{7,3},{8,12},{9,13},{10,... | collective-permute-start | bytes 786440 | tf_op jit(solution)/shard_map/ppermute | solution.py:507
  78.5 13.3 %collective-permute-start.15 = (bf16[2,2,2,128,128]{4,3,2,1,0:T(8,128)(2,1)S(1)}, bf16[2,2,2,128,128]{4,3,2,1,0:T(8,128)(2,1)S(1)}, u32[]{:S(2)}, u32[]{:S(2)}) collective-permute-start(bf16[2,2,2,128,128]{4,3,2,1,0:T(8,128)(2,1)S(1)} %add_convert_fusion), channel_id=1, source_target_pairs={{0,2},{1,3},{2,0},{3,1},{4,6},{5,7},{6,4},{7,5},{8,10},{9,11},{10,... | collective-permute-start | bytes 786440 | tf_op jit(solution)/shard_map/ppermute | solution.py:507
  86.5 8.2 %collective-permute-start.13 = (bf16[2,128,1024]{2,1,0:T(8,128)(2,1)S(1)}, bf16[2,128,1024]{2,1,0:T(8,128)(2,1)S(1)}, u32[]{:S(2)}, u32[]{:S(2)}) collective-permute-start(bf16[2,128,1024]{2,1,0:T(8,128)(2,1)S(1)} %get-tuple-element.89), channel_id=1, source_target_pairs={{0,1},{1,0},{2,3},{3,2},{4,5},{5,4},{6,7},{7,6},{8,9},{9,8},{10,11... | collective-permute-start | bytes 1572872 | tf_op jit(solution)/shard_map/ppermute | solution.py:507
  91.6 3.1 %collective-permute-start.14 = (bf16[2,128,1024]{2,1,0:T(8,128)(2,1)S(1)}, bf16[2,128,1024]{2,1,0:T(8,128)(2,1)S(1)}, u32[]{:S(2)}, u32[]{:S(2)}) collective-permute-start(bf16[2,128,1024]{2,1,0:T(8,128)(2,1)S(1)} %get-tuple-element.90), channel_id=1, source_target_pairs={{0,1},{1,0},{2,3},{3,2},{4,5},{5,4},{6,7},{7,6},{8,9},{9,8},{10,11... | collective-permute-start | bytes 1572872 | tf_op jit(solution)/shard_map/ppermute | solution.py:507
  92.6 2.1 %collective-permute-start.17 = (bf16[2,128,256]{2,1,0:T(8,128)(2,1)S(1)}, bf16[2,128,256]{2,1,0:T(8,128)(2,1)S(1)}, u32[]{:S(2)}, u32[]{:S(2)}) collective-permute-start(bf16[2,128,256]{2,1,0:T(8,128)(2,1)S(1)} %get-tuple-element.95), channel_id=1, source_target_pairs={{0,1},{1,0},{2,3},{3,2},{4,5},{5,4},{6,7},{7,6},{8,9},{9,8},{10,11... | collective-permute-start | bytes 393224 | tf_op jit(solution)/shard_map/ppermute | solution.py:507
where the time goes:
time: 97.4 us; the launch traced here: 96.2 us
  starting transfers between devices  36.6 us (38%)
  Pallas kernels  35.5 us (36%)
  waiting for transfers between devices  21.7 us (22%)
  local copies, waits for them, and re-layouts  1.31 us (1%)
    pallas_call x10, Pallas kernels, run(): pl.pallas_call(kernel, out_shape=[placed(n, a) for n, a in enumerate(outs...  35.5 us
    ppermute x13, starting transfers between devices, cross(): return lax.ppermute(array, 'seq', [(m, m ^ by) for m in range(n_seq)])  19.9 us
    ppermute x3, waiting for transfers between devices, onward(): return lax.ppermute(array, 'grp', [(g, g + 1) for g in range(n_grp - 1)])  10.4 us
    ppermute x2, starting transfers between devices, back(): return lax.ppermute(array, 'grp', [(g + 1, g) for g in range(n_grp - 1)])  9.83 us
    ppermute x13, waiting for transfers between devices, cross(): return lax.ppermute(array, 'seq', [(m, m ^ by) for m in range(n_seq)])  7.58 us
    ppermute x3, starting transfers between devices, onward(): return lax.ppermute(array, 'grp', [(g, g + 1) for g in range(n_grp - 1)])  6.94 us
    ppermute x2, waiting for transfers between devices, back(): return lax.ppermute(array, 'grp', [(g + 1, g) for g in range(n_grp - 1)])  3.74 us
  transfers between devices with their start and end apart: 18, of which 7 were waited for; matrix products, arithmetic and copies ran while one was open for 1% of the time, Pallas kernels for 19%

commit v1 on v0

--- a/solution.py
+++ b/solution.py
@@ -405,56 +405,53 @@
     outs, (store, low, out_acc, dq_acc, got) = rest[: 2 * HALF_KV], rest[2 * HALF_KV :]
     group, member, _ = here(n_seq)
 
-    def copy(source, h, i, n, first):
-        return pltpu.make_async_copy(source.at[i, n - first, h], low.at[h, i, n], got.at[h, i, n])
-
-    ends = []
+    def copy(source, i, n, first):
+        return pltpu.make_async_copy(source.at[i, n - first], low.at[i, n], got.at[i, n])
+
+    totals = []
     for i in range(2):
-        stops = [0]
-        for section in range(n_saved):
-            stops.append(stops[-1] + counts[i, section])
-        ends.append(stops)
-    for h in range(HALF_KV):
-        for i, stops in enumerate(ends):
-            for source, first, stop in zip(saved, stops, stops[1:]):
-
-                def fetch_one(n, _):
-                    copy(source, h, i, n, first).start()
-                    return 0
-
-                lax.fori_loop(first, stop, fetch_one, 0)
+        first = 0
+        for section, source in enumerate(saved):
+            stop = first + counts[i, section]
+
+            def fetch_one(n, _):
+                copy(source, i, n, first).start()
+                return 0
+
+            lax.fori_loop(first, stop, fetch_one, 0)
+            first = stop
+        totals.append(first)
     fill(store, pieces)
     tables = []
     for i in range(2):
         mine = group * n_seq + lax.bitwise_xor(member, i)
         cosine, sine = block_tables(place_ref[mine], table)
         tables.append((cosine.T * SCALE, sine.T * SCALE))
-    for h, (i, stops) in ((h, pair) for h in range(HALF_KV) for pair in enumerate(ends)):
-        total = stops[-1]
+    for h, (i, total) in ((h, pair) for h in range(HALF_KV) for pair in enumerate(totals)):
         result = outs[i * HALF_KV + h]
 
         @pl.when(lax.rem(total, 2) == 1)
         def _():
-            low[h, i, total] = jnp.zeros((2, BLK, ROWS), BF16)
+            low[i, total, h] = jnp.zeros((2, BLK, ROWS), BF16)
 
         out_acc[...] = jnp.zeros_like(out_acc)
         dq_acc[...] = jnp.zeros_like(dq_acc)
 
         def add(n, _):
             pair = (2 * n, 2 * n + 1)
-            for m in pair:
-                for source, first, stop in zip(saved, stops, stops[1:]):
-
-                    @pl.when(jnp.logical_and(m >= first, m < stop))
+            if h == 0:
+                for m in pair:
+
+                    @pl.when(m < total)
                     def _():
-                        copy(source, h, i, m, first).wait()
+                        copy(saved[0], i, m, m).wait()
 
             found = [lists[i, 3, m] for m in pair]
             keys_t = jnp.concatenate([store[e, 0, h].T for e in found], axis=1)
             values_t = jnp.concatenate([store[e, 1, h].T for e in found], axis=1)
             for _, columns in chunks():
-                probs = jnp.concatenate([low[h, i, m, 0, :, columns] for m in pair], axis=0)
-                dscores = jnp.concatenate([low[h, i, m, 1, :, columns] for m in pair], axis=0)
+                probs = jnp.concatenate([low[i, m, h, 0, :, columns] for m in pair], axis=0)
+                dscores = jnp.concatenate([low[i, m, h, 1, :, columns] for m in pair], axis=0)
                 out_acc[:, columns] += dot_nn(values_t, probs)
                 dq_acc[:, columns] += dot_nn(keys_t, dscores)
             return 0
@@ -622,11 +619,11 @@
     half_out = jax.ShapeDtypeStruct((2, BLK, RATIO * HEAD_DIM), BF16)
     place_late, _ = lax.optimization_barrier((block_position, merged))
     wide = pltpu.VMEM((HEAD_DIM, ROWS), F32)
-    slots = (HALF_KV, 2, n_listed + 1)
+    slots = (2, n_listed + 1)
     halves = call(
         functools.partial(query_results, n_seq), (half_out,) * (2 * HALF_KV), 3,
         [
-            pltpu.VMEM((2 * n_seq, *piece), BF16), pltpu.VMEM((*slots, 2, BLK, ROWS), BF16),
+            pltpu.VMEM((2 * n_seq, *piece), BF16), pltpu.VMEM((*slots, HALF_KV, 2, BLK, ROWS), BF16),
             wide, wide, pltpu.SemaphoreType.DMA(slots),
         ],
         us=20, name="query_results", n_hbm=3,

time: 97.4 us -> 101 us (1.037)
  Pallas kernels: 35.5 us -> 46.7 us
  starting transfers between devices: 36.6 us -> 25.6 us
  waiting for transfers between devices: 21.7 us -> 24.9 us
    pallas_call x10, Pallas kernels: 35.5 us -> 46.7 us  [run(): pl.pallas_call(kernel, out_shape=[placed(n, a) for n, a in enumerate(outs...]
    ppermute x2, starting transfers between devices: 9.83 us -> 3.97 us  [back(): return lax.ppermute(array, 'grp', [(g + 1, g) for g in range(n_grp - 1)])]
    ppermute x13, starting transfers between devices: 19.9 us -> 14.7 us  [cross(): return lax.ppermute(array, 'seq', [(m, m ^ by) for m in range(n_seq)])]
    ppermute x13, waiting for transfers between devices: 7.58 us -> 9.86 us  [cross(): return lax.ppermute(array, 'seq', [(m, m ^ by) for m in range(n_seq)])]
    ppermute x2, waiting for transfers between devices: 3.74 us -> 5.39 us  [back(): return lax.ppermute(array, 'grp', [(g + 1, g) for g in range(n_grp - 1)])]
  transfers between devices with their start and end apart: 18 -> 18, of which waited for: 7 -> 8; matrix products, arithmetic and copies ran while one was open for 1% -> 1% of each run, Pallas kernels for 19% -> 24%
where the time goes in v1:
time: 101 us; the launch traced here: 99.7 us
  Pallas kernels  46.7 us (46%)
  starting transfers between devices  25.6 us (25%)
  waiting for transfers between devices  24.9 us (25%)
  local copies, waits for them, and re-layouts  1.31 us (1%)
    pallas_call x10, Pallas kernels, run(): pl.pallas_call(kernel, out_shape=[placed(n, a) for n, a in enumerate(outs...  46.7 us
    ppermute x13, starting transfers between devices, cross(): return lax.ppermute(array, 'seq', [(m, m ^ by) for m in range(n_seq)])  14.7 us
    ppermute x13, waiting for transfers between devices, cross(): return lax.ppermute(array, 'seq', [(m, m ^ by) for m in range(n_seq)])  9.86 us
    ppermute x3, waiting for transfers between devices, onward(): return lax.ppermute(array, 'grp', [(g, g + 1) for g in range(n_grp - 1)])  9.67 us
    ppermute x3, starting transfers between devices, onward(): return lax.ppermute(array, 'grp', [(g, g + 1) for g in range(n_grp - 1)])  6.94 us
    ppermute x2, waiting for transfers between devices, back(): return lax.ppermute(array, 'grp', [(g + 1, g) for g in range(n_grp - 1)])  5.39 us
    ppermute x2, starting transfers between devices, back(): return lax.ppermute(array, 'grp', [(g + 1, g) for g in range(n_grp - 1)])  3.97 us
  transfers between devices with their start and end apart: 18, of which 8 were waited for; matrix products, arithmetic and copies ran while one was open for 1% of the time, Pallas kernels for 24%

profile of v1, /device:TPU:5, one launch (start us, length us, event | category | flops | bytes accessed | tf_op | source)
XLA Modules:
  0.0 99.7 jit_solution(17319071237451521516)
XLA Ops:
  0.6 0.0 copy-start.4
  0.6 3.5 %prepare.1 = (bf16[2,2,128,128]{3,2,1,0:T(8,128)(2,1)S(1)}, bf16[2,2,128,128]{3,2,1,0:T(8,128)(2,1)S(1)}, bf16[2,2,8,128,128]{4,3,2,1,0:T(8,128)(2,1)}, bf16[2,2,8,128,128]{4,3,2,1,0:T(8,128)(2,1)S(1)}) custom-call(s32[32]{0:T(128)} %place_ref.4, bf16[128,512]{1,0:T(8,128)(2,1)} %refs_0_.1, bf16[128,512]{1,0:T(8,128)(2,1)} %refs_1_.1, ...), custom_call_target="tpu_custom_call" | custom-call | flops 3000000000 | bytes 1048576 | tf_op jit(solution)/shard_map/prepare/pallas_call | solution.py:99
  4.2 0.7 collective-permute-start
  4.9 1.0 collective-permute-done
  5.9 0.4 collective-permute-start.4
  6.3 3.1 %collective-permute-start.3 = (bf16[2,2,2,128,128]{4,3,2,1,0:T(8,128)(2,1)S(1)}, bf16[2,2,2,128,128]{4,3,2,1,0:T(8,128)(2,1)S(1)}, u32[]{:S(2)}, u32[]{:S(2)}) collective-permute-start(bf16[2,2,2,128,128]{4,3,2,1,0:T(8,128)(2,1)S(1)} %pad_maximum_fusion.rest_0_.rest_7_), channel_id=1, source_target_pairs={{0,8},{8,16},{16,24},{1,9},{9,17},{17,25},{2,10},{10,18},{18,26},{... | collective-permute-start | bytes 786440 | tf_op jit(solution)/shard_map/ppermute | solution.py:510
  9.4 1.4 %collective-permute-start.2 = (bf16[2,2,2,128,128]{4,3,2,1,0:T(8,128)(2,1)S(1)}, bf16[2,2,2,128,128]{4,3,2,1,0:T(8,128)(2,1)S(1)}, u32[]{:S(2)}, u32[]{:S(2)}) collective-permute-start(bf16[2,2,2,128,128]{4,3,2,1,0:T(8,128)(2,1)S(1)} %pad_maximum_fusion.rest_0_.rest_7_), channel_id=1, source_target_pairs={{0,2},{1,3},{2,0},{3,1},{4,6},{5,7},{6,4},{7,5},{8,10},{9,11},{10,... | collective-permute-start | bytes 786440 | tf_op jit(solution)/shard_map/ppermute | solution.py:504
  10.8 2.3 %collective-permute-start.1 = (bf16[2,2,2,128,128]{4,3,2,1,0:T(8,128)(2,1)S(1)}, bf16[2,2,2,128,128]{4,3,2,1,0:T(8,128)(2,1)S(1)}, u32[]{:S(2)}, u32[]{:S(2)}) collective-permute-start(bf16[2,2,2,128,128]{4,3,2,1,0:T(8,128)(2,1)S(1)} %pad_maximum_fusion.rest_0_.rest_7_), channel_id=1, source_target_pairs={{0,4},{1,5},{2,6},{3,7},{4,0},{5,1},{6,2},{7,3},{8,12},{9,13},{10,... | collective-permute-start | bytes 786440 | tf_op jit(solution)/shard_map/ppermute | solution.py:504
  13.1 0.0 copy-done.4
  13.1 0.7 copy.12.key_blocks
  13.8 2.1 %block_lists.1 = (s32[2,4,13]{2,1,0:T(4,128)S(1)}, s32[2,4]{1,0:T(2,128)S(1)}) custom-call(s32[32,12]{1,0:T(8,128)} %copy.12.key_blocks, s32[32]{0:T(128)} %key_counts.1), custom_call_target="tpu_custom_call" | custom-call | flops 2000000000 | bytes 1048576 | tf_op jit(solution)/shard_map/block_lists/pallas_call | solution.py:99
  15.9 0.0 copy-start.2
  15.9 0.6 copy-done.2
  16.5 0.0 copy-start.3
  16.5 0.0 copy-start.1
  16.5 0.4 collective-permute-done.3.rest_0_.rest_3_
  16.9 5.6 %collective-permute-done.2.rest_1_.rest_8_ = bf16[2,2,2,128,128]{4,3,2,1,0:T(8,128)(2,1)S(1)} collective-permute-done((bf16[2,2,2,128,128]{4,3,2,1,0:T(8,128)(2,1)S(1)}, bf16[2,2,2,128,128]{4,3,2,1,0:T(8,128)(2,1)S(1)}, u32[]{:S(2)}, u32[]{:S(2)}) %collective-permute-start.2) | collective-permute-done | bytes 262176 | tf_op jit(solution)/shard_map/ppermute | solution.py:504
  22.4 0.0 collective-permute-done.1.rest_1_.rest_0_.rest_9_
  22.5 2.5 %collective-permute-start.6 = (bf16[2,2,2,128,128]{4,3,2,1,0:T(8,128)(2,1)S(1)}, bf16[2,2,2,128,128]{4,3,2,1,0:T(8,128)(2,1)S(1)}, u32[]{:S(2)}, u32[]{:S(2)}) collective-permute-start(bf16[2,2,2,128,128]{4,3,2,1,0:T(8,128)(2,1)S(1)} %collective-permute-done.1.rest_1_.rest_0_.rest_9_), channel_id=1, source_target_pairs={{0,2},{1,3},{2,0},{3,1},{4,6},{5,7},{6,4},{7,5},{8,10},{9,11},{10,... | collective-permute-start | bytes 786440 | tf_op jit(solution)/shard_map/ppermute | solution.py:504
  24.9 1.9 %collective-permute-start.5 = (bf16[2,2,2,128,128]{4,3,2,1,0:T(8,128)(2,1)S(1)}, bf16[2,2,2,128,128]{4,3,2,1,0:T(8,128)(2,1)S(1)}, u32[]{:S(2)}, u32[]{:S(2)}) collective-permute-start(bf16[2,2,2,128,128]{4,3,2,1,0:T(8,128)(2,1)S(1)} %collective-permute-done.1.rest_1_.rest_0_.rest_9_), channel_id=1, source_target_pairs={{0,8},{8,16},{16,24},{1,9},{9,17},{17,25},{2,10},{10,18},{18,26},{... | collective-permute-start | bytes 786440 | tf_op jit(solution)/shard_map/ppermute | solution.py:510
  26.8 0.0 collective-permute-done.4.other
  26.8 0.0 copy-done.3
  26.9 2.9 %near_statistics.1.rest_0_ = f32[2,2,8,1024]{3,2,1,0:T(8,128)S(1)} custom-call(s32[2,4,13]{2,1,0:T(4,128)} %copy-done.2, s32[2,4]{1,0:T(2,128)} %copy-done.3, bf16[2,2,8,128,128]{4,3,2,1,0:T(8,128)(2,1)} %get-tuple-element.59.own, bf16[2,2,8,128,128]{4,3,2,1,0:T(8,128)(2,1)S(1)} %collective-permute-done.4.other, ...), custom_call_target="tpu_custom_call" | custom-call | flops 4000000000 | bytes 1048576 | tf_op jit(solution)/shard_map/near_statistics/pallas_call | solution.py:99
  29.7 4.1 %collective-permute-done.5.rest_2_.rest_5_ = bf16[2,2,2,128,128]{4,3,2,1,0:T(8,128)(2,1)S(1)} collective-permute-done((bf16[2,2,2,128,128]{4,3,2,1,0:T(8,128)(2,1)S(1)}, bf16[2,2,2,128,128]{4,3,2,1,0:T(8,128)(2,1)S(1)}, u32[]{:S(2)}, u32[]{:S(2)}) %collective-permute-start.5) | collective-permute-done | bytes 262176 | tf_op jit(solution)/shard_map/ppermute | solution.py:510
  33.9 1.9 %collective-permute-start.7 = (bf16[2,2,2,128,128]{4,3,2,1,0:T(8,128)(2,1)S(1)}, bf16[2,2,2,128,128]{4,3,2,1,0:T(8,128)(2,1)S(1)}, u32[]{:S(2)}, u32[]{:S(2)}) collective-permute-start(bf16[2,2,2,128,128]{4,3,2,1,0:T(8,128)(2,1)S(1)} %collective-permute-done.2.rest_1_.rest_8_), channel_id=1, source_target_pairs={{0,8},{8,16},{16,24},{1,9},{9,17},{17,25},{2,10},{10,18},{18,26},{... | collective-permute-start | bytes 786440 | tf_op jit(solution)/shard_map/ppermute | solution.py:510
  35.8 0.1 collective-permute-start.8
  35.9 0.0 collective-permute-done.6.rest_2_.rest_1_.rest_10_
  35.9 0.0 copy-done.1
  35.9 0.8 far_statistics.1.stats_in
  36.7 5.2 %collective-permute-done.7.rest_1_.rest_4_ = bf16[2,2,2,128,128]{4,3,2,1,0:T(8,128)(2,1)S(1)} collective-permute-done((bf16[2,2,2,128,128]{4,3,2,1,0:T(8,128)(2,1)S(1)}, bf16[2,2,2,128,128]{4,3,2,1,0:T(8,128)(2,1)S(1)}, u32[]{:S(2)}, u32[]{:S(2)}) %collective-permute-start.7) | collective-permute-done | bytes 262176 | tf_op jit(solution)/shard_map/ppermute | solution.py:510
  41.9 0.0 collective-permute-done.8.rest_3_.rest_6_
  41.9 17.5 %previous_gradients.1 = (bf16[4,2,2,128,128]{4,3,2,1,0:T(8,128)(2,1)S(1)}, bf16[2,2,2,128,128]{4,3,2,1,0:T(8,128)(2,1)S(1)}, bf16[2,2,2,128,128]{4,3,2,1,0:T(8,1...) custom-call(s32[2,4,13]{2,1,0:T(4,128)} %copy-done.2, s32[2,4]{1,0:T(2,128)} %copy-done.3, ...), custom_call_target="tpu_custom_call" | custom-call | flops 14000000000 | bytes 1048576 | tf_op jit(solution)/shard_map/previous_gradients/pallas_call | solution.py:99
  59.4 0.1 collective-permute-start.9
  59.5 1.9 %collective-permute-start.12 = (bf16[4,2,2,128,128]{4,3,2,1,0:T(8,128)(2,1)S(1)}, bf16[4,2,2,128,128]{4,3,2,1,0:T(8,128)(2,1)S(1)}, u32[]{:S(2)}, u32[]{:S(2)}) collective-permute-start(bf16[4,2,2,128,128]{4,3,2,1,0:T(8,128)(2,1)S(1)} %get-tuple-element.83), channel_id=1, source_target_pairs={{8,0},{16,8},{24,16},{9,1},{17,9},{25,17},{10,2},{18,10},{26,18},{... | collective-permute-start | bytes 1572872 | tf_op jit(solution)/shard_map/ppermute | solution.py:513
  61.4 1.0 far_current_gradients.1
  62.4 2.3 %collective-permute-done.9 = bf16[2,2,2,128,128]{4,3,2,1,0:T(8,128)(2,1)S(1)} collective-permute-done((bf16[2,2,2,128,128]{4,3,2,1,0:T(8,128)(2,1)S(1)}, bf16[2,2,2,128,128]{4,3,2,1,0:T(8,128)(2,1)S(1)}, u32[]{:S(2)}, u32[]{:S(2)}) %collective-permute-start.9) | collective-permute-done | bytes 262176 | tf_op jit(solution)/shard_map/ppermute | solution.py:504
  64.7 0.1 add_convert_fusion.2
  64.7 0.0 copy-start
  64.8 2.1 %collective-permute-start.10 = (bf16[2,2,2,128,128]{4,3,2,1,0:T(8,128)(2,1)S(1)}, bf16[2,2,2,128,128]{4,3,2,1,0:T(8,128)(2,1)S(1)}, u32[]{:S(2)}, u32[]{:S(2)}) collective-permute-start(bf16[2,2,2,128,128]{4,3,2,1,0:T(8,128)(2,1)S(1)} %add_convert_fusion.2), channel_id=1, source_target_pairs={{8,0},{16,8},{24,16},{9,1},{17,9},{25,17},{10,2},{18,10},{26,18},{... | collective-permute-start | bytes 786440 | tf_op jit(solution)/shard_map/ppermute | solution.py:513
  66.8 0.1 collective-permute-start.11
  66.9 4.3 %near_current_gradients.1 = (f32[2,2,2,128,128]{4,3,2,1,0:T(8,128)S(1)}, f32[2,2,2,128,128]{4,3,2,1,0:T(8,128)S(1)}, bf16[2,4,2,2,128,1024]{5,4,3,2,1,0:T(8,128)(2,1)}) custom-call(s32[2,4,13]{2,1,0:T(4,128)} %copy-done.2, s32[2,4]{1,0:T(2,128)} %copy-done.3, bf16[2,2,8,128,128]{4,3,2,1,0:T(8,128)(2,1)S(1)} %copy-done.1, ...), custom_call_target="tpu_custom_call" | custom-call | flops 6000000000 | bytes 1048576 | tf_op jit(solution)/shard_map/near_current_gradients/pallas_call | solution.py:99
  71.2 5.4 %collective-permute-done.10 = bf16[2,2,2,128,128]{4,3,2,1,0:T(8,128)(2,1)S(1)} collective-permute-done((bf16[2,2,2,128,128]{4,3,2,1,0:T(8,128)(2,1)S(1)}, bf16[2,2,2,128,128]{4,3,2,1,0:T(8,128)(2,1)S(1)}, u32[]{:S(2)}, u32[]{:S(2)}) %collective-permute-start.10) | collective-permute-done | bytes 262176 | tf_op jit(solution)/shard_map/ppermute | solution.py:513
  76.5 0.0 collective-permute-done.11
  76.6 0.1 add_convert_fusion.1
  76.6 0.1 collective-permute-start.16
  76.7 0.0 collective-permute-done.12
  76.7 0.1 add_convert_fusion
  76.8 1.2 %collective-permute-start.15 = (bf16[2,2,2,128,128]{4,3,2,1,0:T(8,128)(2,1)S(1)}, bf16[2,2,2,128,128]{4,3,2,1,0:T(8,128)(2,1)S(1)}, u32[]{:S(2)}, u32[]{:S(2)}) collective-permute-start(bf16[2,2,2,128,128]{4,3,2,1,0:T(8,128)(2,1)S(1)} %add_convert_fusion), channel_id=1, source_target_pairs={{0,2},{1,3},{2,0},{3,1},{4,6},{5,7},{6,4},{7,5},{8,10},{9,11},{10,... | collective-permute-start | bytes 786440 | tf_op jit(solution)/shard_map/ppermute | solution.py:504
  78.0 0.0 copy-done
  78.0 12.2 %query_results.1 = (bf16[2,128,1024]{2,1,0:T(8,128)(2,1)S(1)}, bf16[2,128,1024]{2,1,0:T(8,128)(2,1)S(1)}, bf16[2,128,1024]{2,1,0:T(8,128)(2,1)S(1)}, bf16[2,128,1024]{2,1,0:T(8,128)(2,1)S(1)}) custom-call(s32[2,4,13]{2,1,0:T(4,128)} %copy-done.2, s32[2,4]{1,0:T(2,128)} %copy-done.3, s32[32]{0:T(128)} %place_ref.4, ...), custom_call_target="tpu_custom_call" | custom-call | flops 20000000000 | bytes 1048576 | tf_op jit(solution)/shard_map/query_results/pallas_call | solution.py:99
  90.2 5.4 %collective-permute-start.13 = (bf16[2,128,1024]{2,1,0:T(8,128)(2,1)S(1)}, bf16[2,128,1024]{2,1,0:T(8,128)(2,1)S(1)}, u32[]{:S(2)}, u32[]{:S(2)}) collective-permute-start(bf16[2,128,1024]{2,1,0:T(8,128)(2,1)S(1)} %get-tuple-element.89), channel_id=1, source_target_pairs={{0,1},{1,0},{2,3},{3,2},{4,5},{5,4},{6,7},{7,6},{8,9},{9,8},{10,11... | collective-permute-start | bytes 1572872 | tf_op jit(solution)/shard_map/ppermute | solution.py:504
  95.7 0.1 collective-permute-start.14
  95.8 0.0 collective-permute-done.16.rest_3_
  95.8 0.0 collective-permute-done.15.rest_2_
  95.8 0.9 key_gradients.1
  96.7 0.5 collective-permute-start.17
  97.2 1.0 collective-permute-done.17.refs_5_
  98.1 0.0 collective-permute-done.13.refs_2_
  98.1 0.0 collective-permute-done.14.refs_3_
  98.1 1.6 %join_halves.1 = (bf16[128,4096]{1,0:T(8,128)(2,1)}, bf16[128,4096]{1,0:T(8,128)(2,1)}, bf16[128,512]{1,0:T(8,128)(2,1)}, bf16[128,512]{1,0:T(8,128)(2,1)}) custom-call(bf16[2,128,1024]{2,1,0:T(8,128)(2,1)S(1)} %get-tuple-element.80.refs_0_, bf16[2,128,1024]{2,1,0:T(8,128)(2,1)S(1)} %get-tuple-element.86.refs_1_, ...), custom_call_target="tpu_custom_call" | custom-call | flops 2000000000 | bytes 1048576 | tf_op jit(solution)/shard_map/join_halves/pallas_call | solution.py:99
  (2 shorter events, 0.0 us)
Async XLA Ops:
  0.6 12.5 %copy-start.4 = (s32[32,12]{0,1:T(8,128)S(1)}, s32[32,12]{0,1:T(8,128)}, u32[]{:S(2)}) copy-start(s32[32,12]{0,1:T(8,128)} %param.12) | copy-start | bytes 4612
  4.2 1.7 %collective-permute-start = (bf16[2,2,128,128]{3,2,1,0:T(8,128)(2,1)S(1)}, bf16[2,2,128,128]{3,2,1,0:T(8,128)(2,1)S(1)}, u32[]{:S(2)}, u32[]{:S(2)}) collective-permute-start(bf16[2,2,128,128]{3,2,1,0:T(8,128)(2,1)S(1)} %get-tuple-element.52), channel_id=1, source_target_pairs={{0,1},{1,0},{2,3},{3,2},{4,5},{5,4},{6,7},{7,6},{8,9},{9,8},{10,11... | collective-permute-start | bytes 393224 | tf_op jit(solution)/shard_map/ppermute | solution.py:504
  5.9 20.9 %collective-permute-start.4 = (bf16[2,2,8,128,128]{4,3,2,1,0:T(8,128)(2,1)S(1)}, bf16[2,2,8,128,128]{4,3,2,1,0:T(8,128)(2,1)S(1)}, u32[]{:S(2)}, u32[]{:S(2)}) collective-permute-start(bf16[2,2,8,128,128]{4,3,2,1,0:T(8,128)(2,1)S(1)} %get-tuple-element.60), channel_id=1, source_target_pairs={{0,1},{1,0},{2,3},{3,2},{4,5},{5,4},{6,7},{7,6},{8,9},{9,8},{10,11... | collective-permute-start | bytes 3145736 | tf_op jit(solution)/shard_map/ppermute | solution.py:504
  6.3 10.5 %collective-permute-start.3 = (bf16[2,2,2,128,128]{4,3,2,1,0:T(8,128)(2,1)S(1)}, bf16[2,2,2,128,128]{4,3,2,1,0:T(8,128)(2,1)S(1)}, u32[]{:S(2)}, u32[]{:S(2)}) collective-permute-start(bf16[2,2,2,128,128]{4,3,2,1,0:T(8,128)(2,1)S(1)} %pad_maximum_fusion.rest_0_.rest_7_), channel_id=1, source_target_pairs={{0,8},{8,16},{16,24},{1,9},{9,17},{17,25},{2,10},{10,18},{18,26},{... | collective-permute-start | bytes 786440 | tf_op jit(solution)/shard_map/ppermute | solution.py:510
  9.4 13.0 %collective-permute-start.2 = (bf16[2,2,2,128,128]{4,3,2,1,0:T(8,128)(2,1)S(1)}, bf16[2,2,2,128,128]{4,3,2,1,0:T(8,128)(2,1)S(1)}, u32[]{:S(2)}, u32[]{:S(2)}) collective-permute-start(bf16[2,2,2,128,128]{4,3,2,1,0:T(8,128)(2,1)S(1)} %pad_maximum_fusion.rest_0_.rest_7_), channel_id=1, source_target_pairs={{0,2},{1,3},{2,0},{3,1},{4,6},{5,7},{6,4},{7,5},{8,10},{9,11},{10,... | collective-permute-start | bytes 786440 | tf_op jit(solution)/shard_map/ppermute | solution.py:504
  10.8 11.6 %collective-permute-start.1 = (bf16[2,2,2,128,128]{4,3,2,1,0:T(8,128)(2,1)S(1)}, bf16[2,2,2,128,128]{4,3,2,1,0:T(8,128)(2,1)S(1)}, u32[]{:S(2)}, u32[]{:S(2)}) collective-permute-start(bf16[2,2,2,128,128]{4,3,2,1,0:T(8,128)(2,1)S(1)} %pad_maximum_fusion.rest_0_.rest_7_), channel_id=1, source_target_pairs={{0,4},{1,5},{2,6},{3,7},{4,0},{5,1},{6,2},{7,3},{8,12},{9,13},{10,... | collective-permute-start | bytes 786440 | tf_op jit(solution)/shard_map/ppermute | solution.py:504
  15.9 0.6 copy-start.2
  16.5 10.3 %copy-start.3 = (s32[2,4]{1,0:T(2,128)}, s32[2,4]{1,0:T(2,128)S(1)}, u32[]{:S(2)}) copy-start(s32[2,4]{1,0:T(2,128)S(1)} %get-tuple-element.58.counts) | copy-start | bytes 100
  16.5 19.4 %copy-start.1 = (bf16[2,2,8,128,128]{4,3,2,1,0:T(8,128)(2,1)S(1)}, bf16[2,2,8,128,128]{4,3,2,1,0:T(8,128)(2,1)}, u32[]{:S(2)}) copy-start(bf16[2,2,8,128,128]{4,3,2,1,0:T(8,128)(2,1)} %get-tuple-element.59.own) | copy-start | bytes 3145732
  22.5 13.4 %collective-permute-start.6 = (bf16[2,2,2,128,128]{4,3,2,1,0:T(8,128)(2,1)S(1)}, bf16[2,2,2,128,128]{4,3,2,1,0:T(8,128)(2,1)S(1)}, u32[]{:S(2)}, u32[]{:S(2)}) collective-permute-start(bf16[2,2,2,128,128]{4,3,2,1,0:T(8,128)(2,1)S(1)} %collective-permute-done.1.rest_1_.rest_0_.rest_9_), channel_id=1, source_target_pairs={{0,2},{1,3},{2,0},{3,1},{4,6},{5,7},{6,4},{7,5},{8,10},{9,11},{10,... | collective-permute-start | bytes 786440 | tf_op jit(solution)/shard_map/ppermute | solution.py:504
  24.9 9.0 %collective-permute-start.5 = (bf16[2,2,2,128,128]{4,3,2,1,0:T(8,128)(2,1)S(1)}, bf16[2,2,2,128,128]{4,3,2,1,0:T(8,128)(2,1)S(1)}, u32[]{:S(2)}, u32[]{:S(2)}) collective-permute-start(bf16[2,2,2,128,128]{4,3,2,1,0:T(8,128)(2,1)S(1)} %collective-permute-done.1.rest_1_.rest_0_.rest_9_), channel_id=1, source_target_pairs={{0,8},{8,16},{16,24},{1,9},{9,17},{17,25},{2,10},{10,18},{18,26},{... | collective-permute-start | bytes 786440 | tf_op jit(solution)/shard_map/ppermute | solution.py:510
  33.9 8.0 %collective-permute-start.7 = (bf16[2,2,2,128,128]{4,3,2,1,0:T(8,128)(2,1)S(1)}, bf16[2,2,2,128,128]{4,3,2,1,0:T(8,128)(2,1)S(1)}, u32[]{:S(2)}, u32[]{:S(2)}) collective-permute-start(bf16[2,2,2,128,128]{4,3,2,1,0:T(8,128)(2,1)S(1)} %collective-permute-done.2.rest_1_.rest_8_), channel_id=1, source_target_pairs={{0,8},{8,16},{16,24},{1,9},{9,17},{17,25},{2,10},{10,18},{18,26},{... | collective-permute-start | bytes 786440 | tf_op jit(solution)/shard_map/ppermute | solution.py:510
  35.8 6.1 %collective-permute-start.8 = (bf16[2,2,2,128,128]{4,3,2,1,0:T(8,128)(2,1)S(1)}, bf16[2,2,2,128,128]{4,3,2,1,0:T(8,128)(2,1)S(1)}, u32[]{:S(2)}, u32[]{:S(2)}) collective-permute-start(bf16[2,2,2,128,128]{4,3,2,1,0:T(8,128)(2,1)S(1)} %collective-permute-done.5.rest_2_.rest_5_), channel_id=1, source_target_pairs={{0,2},{1,3},{2,0},{3,1},{4,6},{5,7},{6,4},{7,5},{8,10},{9,11},{10,... | collective-permute-start | bytes 786440 | tf_op jit(solution)/shard_map/ppermute | solution.py:504
  59.4 5.3 %collective-permute-start.9 = (bf16[2,2,2,128,128]{4,3,2,1,0:T(8,128)(2,1)S(1)}, bf16[2,2,2,128,128]{4,3,2,1,0:T(8,128)(2,1)S(1)}, u32[]{:S(2)}, u32[]{:S(2)}) collective-permute-start(bf16[2,2,2,128,128]{4,3,2,1,0:T(8,128)(2,1)S(1)} %get-tuple-element.66), channel_id=1, source_target_pairs={{0,2},{1,3},{2,0},{3,1},{4,6},{5,7},{6,4},{7,5},{8,10},{9,11},{10,... | collective-permute-start | bytes 786440 | tf_op jit(solution)/shard_map/ppermute | solution.py:504
  59.5 17.3 %collective-permute-start.12 = (bf16[4,2,2,128,128]{4,3,2,1,0:T(8,128)(2,1)S(1)}, bf16[4,2,2,128,128]{4,3,2,1,0:T(8,128)(2,1)S(1)}, u32[]{:S(2)}, u32[]{:S(2)}) collective-permute-start(bf16[4,2,2,128,128]{4,3,2,1,0:T(8,128)(2,1)S(1)} %get-tuple-element.83), channel_id=1, source_target_pairs={{8,0},{16,8},{24,16},{9,1},{17,9},{25,17},{10,2},{18,10},{26,18},{... | collective-permute-start | bytes 1572872 | tf_op jit(solution)/shard_map/ppermute | solution.py:513
  64.7 13.3 %copy-start = (f32[320,128]{1,0:T(8,128)S(1)}, f32[320,128]{1,0:T(8,128)}, u32[]{:S(2)}) copy-start(f32[320,128]{1,0:T(8,128)} %constant.2.clone.refs_4_.rest_11_.rest_4_) | copy-start | bytes 491524
  64.8 11.8 %collective-permute-start.10 = (bf16[2,2,2,128,128]{4,3,2,1,0:T(8,128)(2,1)S(1)}, bf16[2,2,2,128,128]{4,3,2,1,0:T(8,128)(2,1)S(1)}, u32[]{:S(2)}, u32[]{:S(2)}) collective-permute-start(bf16[2,2,2,128,128]{4,3,2,1,0:T(8,128)(2,1)S(1)} %add_convert_fusion.2), channel_id=1, source_target_pairs={{8,0},{16,8},{24,16},{9,1},{17,9},{25,17},{10,2},{18,10},{26,18},{... | collective-permute-start | bytes 786440 | tf_op jit(solution)/shard_map/ppermute | solution.py:513
  66.8 9.7 %collective-permute-start.11 = (bf16[2,2,2,128,128]{4,3,2,1,0:T(8,128)(2,1)S(1)}, bf16[2,2,2,128,128]{4,3,2,1,0:T(8,128)(2,1)S(1)}, u32[]{:S(2)}, u32[]{:S(2)}) collective-permute-start(bf16[2,2,2,128,128]{4,3,2,1,0:T(8,128)(2,1)S(1)} %get-tuple-element.74), channel_id=1, source_target_pairs={{0,2},{1,3},{2,0},{3,1},{4,6},{5,7},{6,4},{7,5},{8,10},{9,11},{10,... | collective-permute-start | bytes 786440 | tf_op jit(solution)/shard_map/ppermute | solution.py:504
  76.6 19.1 %collective-permute-start.16 = (bf16[2,2,2,128,128]{4,3,2,1,0:T(8,128)(2,1)S(1)}, bf16[2,2,2,128,128]{4,3,2,1,0:T(8,128)(2,1)S(1)}, u32[]{:S(2)}, u32[]{:S(2)}) collective-permute-start(bf16[2,2,2,128,128]{4,3,2,1,0:T(8,128)(2,1)S(1)} %add_convert_fusion.1), channel_id=1, source_target_pairs={{0,4},{1,5},{2,6},{3,7},{4,0},{5,1},{6,2},{7,3},{8,12},{9,13},{10,... | collective-permute-start | bytes 786440 | tf_op jit(solution)/shard_map/ppermute | solution.py:504
  76.8 19.0 %collective-permute-start.15 = (bf16[2,2,2,128,128]{4,3,2,1,0:T(8,128)(2,1)S(1)}, bf16[2,2,2,128,128]{4,3,2,1,0:T(8,128)(2,1)S(1)}, u32[]{:S(2)}, u32[]{:S(2)}) collective-permute-start(bf16[2,2,2,128,128]{4,3,2,1,0:T(8,128)(2,1)S(1)} %add_convert_fusion), channel_id=1, source_target_pairs={{0,2},{1,3},{2,0},{3,1},{4,6},{5,7},{6,4},{7,5},{8,10},{9,11},{10,... | collective-permute-start | bytes 786440 | tf_op jit(solution)/shard_map/ppermute | solution.py:504
  90.2 7.9 %collective-permute-start.13 = (bf16[2,128,1024]{2,1,0:T(8,128)(2,1)S(1)}, bf16[2,128,1024]{2,1,0:T(8,128)(2,1)S(1)}, u32[]{:S(2)}, u32[]{:S(2)}) collective-permute-start(bf16[2,128,1024]{2,1,0:T(8,128)(2,1)S(1)} %get-tuple-element.89), channel_id=1, source_target_pairs={{0,1},{1,0},{2,3},{3,2},{4,5},{5,4},{6,7},{7,6},{8,9},{9,8},{10,11... | collective-permute-start | bytes 1572872 | tf_op jit(solution)/shard_map/ppermute | solution.py:504
  95.7 2.5 %collective-permute-start.14 = (bf16[2,128,1024]{2,1,0:T(8,128)(2,1)S(1)}, bf16[2,128,1024]{2,1,0:T(8,128)(2,1)S(1)}, u32[]{:S(2)}, u32[]{:S(2)}) collective-permute-start(bf16[2,128,1024]{2,1,0:T(8,128)(2,1)S(1)} %get-tuple-element.90), channel_id=1, source_target_pairs={{0,1},{1,0},{2,3},{3,2},{4,5},{5,4},{6,7},{7,6},{8,9},{9,8},{10,11... | collective-permute-start | bytes 1572872 | tf_op jit(solution)/shard_map/ppermute | solution.py:504
  96.7 1.5 %collective-permute-start.17 = (bf16[2,128,256]{2,1,0:T(8,128)(2,1)S(1)}, bf16[2,128,256]{2,1,0:T(8,128)(2,1)S(1)}, u32[]{:S(2)}, u32[]{:S(2)}) collective-permute-start(bf16[2,128,256]{2,1,0:T(8,128)(2,1)S(1)} %get-tuple-element.95), channel_id=1, source_target_pairs={{0,1},{1,0},{2,3},{3,2},{4,5},{5,4},{6,7},{7,6},{8,9},{9,8},{10,11... | collective-permute-start | bytes 393224 | tf_op jit(solution)/shard_map/ppermute | solution.py:504

commit v2 on v0

--- a/solution.py
+++ b/solution.py
@@ -443,11 +443,10 @@
         def add(n, _):
             pair = (2 * n, 2 * n + 1)
             for m in pair:
-                for source, first, stop in zip(saved, stops, stops[1:]):
-
-                    @pl.when(jnp.logical_and(m >= first, m < stop))
-                    def _():
-                        copy(source, h, i, m, first).wait()
+
+                @pl.when(m < total)
+                def _():
+                    copy(saved[0], h, i, m, m).wait()
 
             found = [lists[i, 3, m] for m in pair]
             keys_t = jnp.concatenate([store[e, 0, h].T for e in found], axis=1)

time: 97.4 us -> 99.4 us (1.021)
  the two profiles are of different devices: /device:TPU:5 before, /device:TPU:27 now
where the time goes in v2:
time: 99.4 us; the launch traced here: 98.3 us
  Pallas kernels  45.5 us (46%)
  starting transfers between devices  33.5 us (34%)
  waiting for transfers between devices  16.9 us (17%)
  local copies, waits for them, and re-layouts  1.31 us (1%)
    pallas_call x10, Pallas kernels, run(): pl.pallas_call(kernel, out_shape=[placed(n, a) for n, a in enumerate(outs...  45.5 us
    ppermute x13, starting transfers between devices, cross(): return lax.ppermute(array, 'seq', [(m, m ^ by) for m in range(n_seq)])  19.3 us
    ppermute x13, waiting for transfers between devices, cross(): return lax.ppermute(array, 'seq', [(m, m ^ by) for m in range(n_seq)])  10.8 us
    ppermute x3, starting transfers between devices, onward(): return lax.ppermute(array, 'grp', [(g, g + 1) for g in range(n_grp - 1)])  10.2 us
    ppermute x3, waiting for transfers between devices, onward(): return lax.ppermute(array, 'grp', [(g, g + 1) for g in range(n_grp - 1)])  3.97 us
    ppermute x2, starting transfers between devices, back(): return lax.ppermute(array, 'grp', [(g + 1, g) for g in range(n_grp - 1)])  3.96 us
    ppermute x2, waiting for transfers between devices, back(): return lax.ppermute(array, 'grp', [(g + 1, g) for g in range(n_grp - 1)])  2.09 us
  transfers between devices with their start and end apart: 18, of which 8 were waited for; matrix products, arithmetic and copies ran while one was open for 1% of the time, Pallas kernels for 31%

profile of v2, /device:TPU:27, one launch (start us, length us, event | category | flops | bytes accessed | tf_op | source)
XLA Modules:
  0.0 98.3 jit_solution(16691752624622929930)
XLA Ops:
  0.6 0.0 copy-start.4
  0.6 3.5 %prepare.1 = (bf16[2,2,128,128]{3,2,1,0:T(8,128)(2,1)S(1)}, bf16[2,2,128,128]{3,2,1,0:T(8,128)(2,1)S(1)}, bf16[2,2,8,128,128]{4,3,2,1,0:T(8,128)(2,1)}, bf16[2,2,8,128,128]{4,3,2,1,0:T(8,128)(2,1)S(1)}) custom-call(s32[32]{0:T(128)} %place_ref.4, bf16[128,512]{1,0:T(8,128)(2,1)} %refs_0_.1, bf16[128,512]{1,0:T(8,128)(2,1)} %refs_1_.1, ...), custom_call_target="tpu_custom_call" | custom-call | flops 3000000000 | bytes 1048576 | tf_op jit(solution)/shard_map/prepare/pallas_call | solution.py:99
  4.2 0.7 collective-permute-start
  4.9 1.0 %collective-permute-done = bf16[2,2,128,128]{3,2,1,0:T(8,128)(2,1)S(1)} collective-permute-done((bf16[2,2,128,128]{3,2,1,0:T(8,128)(2,1)S(1)}, bf16[2,2,128,128]{3,2,1,0:T(8,128)(2,1)S(1)}, u32[]{:S(2)}, u32[]{:S(2)}) %collective-permute-start) | collective-permute-done | bytes 131104 | tf_op jit(solution)/shard_map/ppermute | solution.py:506
  5.9 0.4 collective-permute-start.4
  6.3 3.1 %collective-permute-start.3 = (bf16[2,2,2,128,128]{4,3,2,1,0:T(8,128)(2,1)S(1)}, bf16[2,2,2,128,128]{4,3,2,1,0:T(8,128)(2,1)S(1)}, u32[]{:S(2)}, u32[]{:S(2)}) collective-permute-start(bf16[2,2,2,128,128]{4,3,2,1,0:T(8,128)(2,1)S(1)} %pad_maximum_fusion.rest_0_.rest_7_), channel_id=1, source_target_pairs={{0,8},{8,16},{16,24},{1,9},{9,17},{17,25},{2,10},{10,18},{18,26},{... | collective-permute-start | bytes 786440 | tf_op jit(solution)/shard_map/ppermute | solution.py:512
  9.4 0.2 collective-permute-start.2
  9.7 0.1 collective-permute-start.1
  9.7 0.0 copy-done.4
  9.7 0.7 copy.12.key_blocks
  10.4 2.0 %block_lists.1 = (s32[2,4,13]{2,1,0:T(4,128)S(1)}, s32[2,4]{1,0:T(2,128)S(1)}) custom-call(s32[32,12]{1,0:T(8,128)} %copy.12.key_blocks, s32[32]{0:T(128)} %key_counts.1), custom_call_target="tpu_custom_call" | custom-call | flops 2000000000 | bytes 1048576 | tf_op jit(solution)/shard_map/block_lists/pallas_call | solution.py:99
  12.5 0.0 copy-start.2
  12.5 0.6 copy-done.2
  13.1 0.0 copy-start.3
  13.1 0.0 copy-start.1
  13.1 2.9 %collective-permute-done.3.rest_0_.rest_3_ = bf16[2,2,2,128,128]{4,3,2,1,0:T(8,128)(2,1)S(1)} collective-permute-done((bf16[2,2,2,128,128]{4,3,2,1,0:T(8,128)(2,1)S(1)}, bf16[2,2,2,128,128]{4,3,2,1,0:T(8,128)(2,1)S(1)}, u32[]{:S(2)}, u32[]{:S(2)}) %collective-permute-start.3) | collective-permute-done | bytes 262176 | tf_op jit(solution)/shard_map/ppermute | solution.py:512
  16.0 5.4 %collective-permute-done.2.rest_1_.rest_8_ = bf16[2,2,2,128,128]{4,3,2,1,0:T(8,128)(2,1)S(1)} collective-permute-done((bf16[2,2,2,128,128]{4,3,2,1,0:T(8,128)(2,1)S(1)}, bf16[2,2,2,128,128]{4,3,2,1,0:T(8,128)(2,1)S(1)}, u32[]{:S(2)}, u32[]{:S(2)}) %collective-permute-start.2) | collective-permute-done | bytes 262176 | tf_op jit(solution)/shard_map/ppermute | solution.py:506
  21.3 2.1 %collective-permute-done.1.rest_1_.rest_0_.rest_9_ = bf16[2,2,2,128,128]{4,3,2,1,0:T(8,128)(2,1)S(1)} collective-permute-done((bf16[2,2,2,128,128]{4,3,2,1,0:T(8,128)(2,1)S(1)}, bf16[2,2,2,128,128]{4,3,2,1,0:T(8,128)(2,1)S(1)}, u32[]{:S(2)}, u32[]{:S(2)}) %collective-permute-start.1) | collective-permute-done | bytes 262176 | tf_op jit(solution)/shard_map/ppermute | solution.py:506
  23.4 0.0 collective-permute-start.6
  23.4 3.1 %collective-permute-start.5 = (bf16[2,2,2,128,128]{4,3,2,1,0:T(8,128)(2,1)S(1)}, bf16[2,2,2,128,128]{4,3,2,1,0:T(8,128)(2,1)S(1)}, u32[]{:S(2)}, u32[]{:S(2)}) collective-permute-start(bf16[2,2,2,128,128]{4,3,2,1,0:T(8,128)(2,1)S(1)} %collective-permute-done.1.rest_1_.rest_0_.rest_9_), channel_id=1, source_target_pairs={{0,8},{8,16},{16,24},{1,9},{9,17},{17,25},{2,10},{10,18},{18,26},{... | collective-permute-start | bytes 786440 | tf_op jit(solution)/shard_map/ppermute | solution.py:512
  26.5 0.0 collective-permute-done.4.other
  26.5 0.0 copy-done.3
  26.5 3.9 %near_statistics.1.rest_0_ = f32[2,2,8,1024]{3,2,1,0:T(8,128)S(1)} custom-call(s32[2,4,13]{2,1,0:T(4,128)} %copy-done.2, s32[2,4]{1,0:T(2,128)} %copy-done.3, bf16[2,2,8,128,128]{4,3,2,1,0:T(8,128)(2,1)} %get-tuple-element.59.own, bf16[2,2,8,128,128]{4,3,2,1,0:T(8,128)(2,1)S(1)} %collective-permute-done.4.other, ...), custom_call_target="tpu_custom_call" | custom-call | flops 4000000000 | bytes 1048576 | tf_op jit(solution)/shard_map/near_statistics/pallas_call | solution.py:99
  30.5 1.1 %collective-permute-done.5.rest_2_.rest_5_ = bf16[2,2,2,128,128]{4,3,2,1,0:T(8,128)(2,1)S(1)} collective-permute-done((bf16[2,2,2,128,128]{4,3,2,1,0:T(8,128)(2,1)S(1)}, bf16[2,2,2,128,128]{4,3,2,1,0:T(8,128)(2,1)S(1)}, u32[]{:S(2)}, u32[]{:S(2)}) %collective-permute-start.5) | collective-permute-done | bytes 262176 | tf_op jit(solution)/shard_map/ppermute | solution.py:512
  31.5 4.0 %collective-permute-start.7 = (bf16[2,2,2,128,128]{4,3,2,1,0:T(8,128)(2,1)S(1)}, bf16[2,2,2,128,128]{4,3,2,1,0:T(8,128)(2,1)S(1)}, u32[]{:S(2)}, u32[]{:S(2)}) collective-permute-start(bf16[2,2,2,128,128]{4,3,2,1,0:T(8,128)(2,1)S(1)} %collective-permute-done.2.rest_1_.rest_8_), channel_id=1, source_target_pairs={{0,8},{8,16},{16,24},{1,9},{9,17},{17,25},{2,10},{10,18},{18,26},{... | collective-permute-start | bytes 786440 | tf_op jit(solution)/shard_map/ppermute | solution.py:512
  35.5 1.2 %collective-permute-start.8 = (bf16[2,2,2,128,128]{4,3,2,1,0:T(8,128)(2,1)S(1)}, bf16[2,2,2,128,128]{4,3,2,1,0:T(8,128)(2,1)S(1)}, u32[]{:S(2)}, u32[]{:S(2)}) collective-permute-start(bf16[2,2,2,128,128]{4,3,2,1,0:T(8,128)(2,1)S(1)} %collective-permute-done.5.rest_2_.rest_5_), channel_id=1, source_target_pairs={{0,2},{1,3},{2,0},{3,1},{4,6},{5,7},{6,4},{7,5},{8,10},{9,11},{10,... | collective-permute-start | bytes 786440 | tf_op jit(solution)/shard_map/ppermute | solution.py:506
  36.8 0.0 collective-permute-done.6.rest_2_.rest_1_.rest_10_
  36.8 0.0 copy-done.1
  36.8 2.9 %far_statistics.1.stats_in = f32[2,2,8,1024]{3,2,1,0:T(8,128)S(1)} custom-call(s32[2,4,13]{2,1,0:T(4,128)} %copy-done.2, s32[2,4]{1,0:T(2,128)} %copy-done.3, bf16[2,2,8,128,128]{4,3,2,1,0:T(8,128)(2,1)S(1)} %copy-done.1, bf16[2,2,8,128,128]{4,3,2,1,0:T(8,128)(2,1)S(1)} %collective-permute-done.4.other, f32[2,2,8,1024]{3,2,1,0:T(8,128)S(1)} %near_statistics.1.rest_0_, ...), custom_call_target="tpu_custom_call" | custom-call | flops 4000000000 | bytes 1048576 | tf_op jit(solution)/shard_map/far_statistics/pallas_call | solution.py:99
  39.7 0.0 collective-permute-done.7.rest_1_.rest_4_
  39.7 1.4 %collective-permute-done.8.rest_3_.rest_6_ = bf16[2,2,2,128,128]{4,3,2,1,0:T(8,128)(2,1)S(1)} collective-permute-done((bf16[2,2,2,128,128]{4,3,2,1,0:T(8,128)(2,1)S(1)}, bf16[2,2,2,128,128]{4,3,2,1,0:T(8,128)(2,1)S(1)}, u32[]{:S(2)}, u32[]{:S(2)}) %collective-permute-start.8) | collective-permute-done | bytes 262176 | tf_op jit(solution)/shard_map/ppermute | solution.py:506
  41.1 9.7 %previous_gradients.1 = (bf16[4,2,2,128,128]{4,3,2,1,0:T(8,128)(2,1)S(1)}, bf16[2,2,2,128,128]{4,3,2,1,0:T(8,128)(2,1)S(1)}, bf16[2,2,2,128,128]{4,3,2,1,0:T(8,1...) custom-call(s32[2,4,13]{2,1,0:T(4,128)} %copy-done.2, s32[2,4]{1,0:T(2,128)} %copy-done.3, ...), custom_call_target="tpu_custom_call" | custom-call | flops 14000000000 | bytes 1048576 | tf_op jit(solution)/shard_map/previous_gradients/pallas_call | solution.py:99
  50.8 4.2 %collective-permute-start.9 = (bf16[2,2,2,128,128]{4,3,2,1,0:T(8,128)(2,1)S(1)}, bf16[2,2,2,128,128]{4,3,2,1,0:T(8,128)(2,1)S(1)}, u32[]{:S(2)}, u32[]{:S(2)}) collective-permute-start(bf16[2,2,2,128,128]{4,3,2,1,0:T(8,128)(2,1)S(1)} %get-tuple-element.66), channel_id=1, source_target_pairs={{0,2},{1,3},{2,0},{3,1},{4,6},{5,7},{6,4},{7,5},{8,10},{9,11},{10,... | collective-permute-start | bytes 786440 | tf_op jit(solution)/shard_map/ppermute | solution.py:506
  55.0 1.9 %collective-permute-start.12 = (bf16[4,2,2,128,128]{4,3,2,1,0:T(8,128)(2,1)S(1)}, bf16[4,2,2,128,128]{4,3,2,1,0:T(8,128)(2,1)S(1)}, u32[]{:S(2)}, u32[]{:S(2)}) collective-permute-start(bf16[4,2,2,128,128]{4,3,2,1,0:T(8,128)(2,1)S(1)} %get-tuple-element.83), channel_id=1, source_target_pairs={{8,0},{16,8},{24,16},{9,1},{17,9},{25,17},{10,2},{18,10},{26,18},{... | collective-permute-start | bytes 1572872 | tf_op jit(solution)/shard_map/ppermute | solution.py:515
  56.9 5.1 %far_current_gradients.1 = (f32[2,2,2,128,128]{4,3,2,1,0:T(8,128)S(1)}, bf16[2,2,2,128,128]{4,3,2,1,0:T(8,128)(2,1)S(1)}, bf16[2,4,2,2,128,1024]{5,4,3,2,1,0:T(8,128)(2,1)}) custom-call(s32[2,4,13]{2,1,0:T(4,128)} %copy-done.2, s32[2,4]{1,0:T(2,128)} %copy-done.3, bf16[2,2,8,128,128]{4,3,2,1,0:T(8,128)(2,1)S(1)} %copy-done.1, ...), custom_call_target="tpu_custom_call" | custom-call | flops 6000000000 | bytes 1048576 | tf_op jit(solution)/shard_map/far_current_gradients/pallas_call | solution.py:99
  62.0 0.0 collective-permute-done.9
  62.0 0.1 add_convert_fusion.2
  62.1 0.0 copy-start
  62.1 2.1 %collective-permute-start.10 = (bf16[2,2,2,128,128]{4,3,2,1,0:T(8,128)(2,1)S(1)}, bf16[2,2,2,128,128]{4,3,2,1,0:T(8,128)(2,1)S(1)}, u32[]{:S(2)}, u32[]{:S(2)}) collective-permute-start(bf16[2,2,2,128,128]{4,3,2,1,0:T(8,128)(2,1)S(1)} %add_convert_fusion.2), channel_id=1, source_target_pairs={{8,0},{16,8},{24,16},{9,1},{17,9},{25,17},{10,2},{18,10},{26,18},{... | collective-permute-start | bytes 786440 | tf_op jit(solution)/shard_map/ppermute | solution.py:515
  64.1 1.3 %collective-permute-start.11 = (bf16[2,2,2,128,128]{4,3,2,1,0:T(8,128)(2,1)S(1)}, bf16[2,2,2,128,128]{4,3,2,1,0:T(8,128)(2,1)S(1)}, u32[]{:S(2)}, u32[]{:S(2)}) collective-permute-start(bf16[2,2,2,128,128]{4,3,2,1,0:T(8,128)(2,1)S(1)} %get-tuple-element.74), channel_id=1, source_target_pairs={{0,2},{1,3},{2,0},{3,1},{4,6},{5,7},{6,4},{7,5},{8,10},{9,11},{10,... | collective-permute-start | bytes 786440 | tf_op jit(solution)/shard_map/ppermute | solution.py:506
  65.4 5.9 %near_current_gradients.1 = (f32[2,2,2,128,128]{4,3,2,1,0:T(8,128)S(1)}, f32[2,2,2,128,128]{4,3,2,1,0:T(8,128)S(1)}, bf16[2,4,2,2,128,1024]{5,4,3,2,1,0:T(8,128)(2,1)}) custom-call(s32[2,4,13]{2,1,0:T(4,128)} %copy-done.2, s32[2,4]{1,0:T(2,128)} %copy-done.3, bf16[2,2,8,128,128]{4,3,2,1,0:T(8,128)(2,1)S(1)} %copy-done.1, ...), custom_call_target="tpu_custom_call" | custom-call | flops 6000000000 | bytes 1048576 | tf_op jit(solution)/shard_map/near_current_gradients/pallas_call | solution.py:99
  71.3 2.1 %collective-permute-done.10 = bf16[2,2,2,128,128]{4,3,2,1,0:T(8,128)(2,1)S(1)} collective-permute-done((bf16[2,2,2,128,128]{4,3,2,1,0:T(8,128)(2,1)S(1)}, bf16[2,2,2,128,128]{4,3,2,1,0:T(8,128)(2,1)S(1)}, u32[]{:S(2)}, u32[]{:S(2)}) %collective-permute-start.10) | collective-permute-done | bytes 262176 | tf_op jit(solution)/shard_map/ppermute | solution.py:515
  73.4 0.0 collective-permute-done.11
  73.4 0.1 add_convert_fusion.1
  73.5 5.2 %collective-permute-start.16 = (bf16[2,2,2,128,128]{4,3,2,1,0:T(8,128)(2,1)S(1)}, bf16[2,2,2,128,128]{4,3,2,1,0:T(8,128)(2,1)S(1)}, u32[]{:S(2)}, u32[]{:S(2)}) collective-permute-start(bf16[2,2,2,128,128]{4,3,2,1,0:T(8,128)(2,1)S(1)} %add_convert_fusion.1), channel_id=1, source_target_pairs={{0,4},{1,5},{2,6},{3,7},{4,0},{5,1},{6,2},{7,3},{8,12},{9,13},{10,... | collective-permute-start | bytes 786440 | tf_op jit(solution)/shard_map/ppermute | solution.py:506
  78.7 0.0 collective-permute-done.12
  78.7 0.1 add_convert_fusion
  78.7 0.4 collective-permute-start.15
  79.1 0.0 copy-done
  79.1 10.0 %query_results.1 = (bf16[2,128,1024]{2,1,0:T(8,128)(2,1)S(1)}, bf16[2,128,1024]{2,1,0:T(8,128)(2,1)S(1)}, bf16[2,128,1024]{2,1,0:T(8,128)(2,1)S(1)}, bf16[2,128,1024]{2,1,0:T(8,128)(2,1)S(1)}) custom-call(s32[2,4,13]{2,1,0:T(4,128)} %copy-done.2, s32[2,4]{1,0:T(2,128)} %copy-done.3, s32[32]{0:T(128)} %place_ref.4, ...), custom_call_target="tpu_custom_call" | custom-call | flops 20000000000 | bytes 1048576 | tf_op jit(solution)/shard_map/query_results/pallas_call | solution.py:99
  89.2 5.1 %collective-permute-start.13 = (bf16[2,128,1024]{2,1,0:T(8,128)(2,1)S(1)}, bf16[2,128,1024]{2,1,0:T(8,128)(2,1)S(1)}, u32[]{:S(2)}, u32[]{:S(2)}) collective-permute-start(bf16[2,128,1024]{2,1,0:T(8,128)(2,1)S(1)} %get-tuple-element.89), channel_id=1, source_target_pairs={{0,1},{1,0},{2,3},{3,2},{4,5},{5,4},{6,7},{7,6},{8,9},{9,8},{10,11... | collective-permute-start | bytes 1572872 | tf_op jit(solution)/shard_map/ppermute | solution.py:506
  94.3 0.1 collective-permute-start.14
  94.4 0.0 collective-permute-done.16.rest_3_
  94.4 0.0 collective-permute-done.15.rest_2_
  94.4 0.9 key_gradients.1
  95.2 0.5 collective-permute-start.17
  95.7 1.0 %collective-permute-done.17.refs_5_ = bf16[2,128,256]{2,1,0:T(8,128)(2,1)S(1)} collective-permute-done((bf16[2,128,256]{2,1,0:T(8,128)(2,1)S(1)}, bf16[2,128,256]{2,1,0:T(8,128)(2,1)S(1)}, u32[]{:S(2)}, u32[]{:S(2)}) %collective-permute-start.17) | collective-permute-done | bytes 131104 | tf_op jit(solution)/shard_map/ppermute | solution.py:506
  96.7 0.0 collective-permute-done.13.refs_2_
  96.7 0.0 collective-permute-done.14.refs_3_
  96.7 1.6 %join_halves.1 = (bf16[128,4096]{1,0:T(8,128)(2,1)}, bf16[128,4096]{1,0:T(8,128)(2,1)}, bf16[128,512]{1,0:T(8,128)(2,1)}, bf16[128,512]{1,0:T(8,128)(2,1)}) custom-call(bf16[2,128,1024]{2,1,0:T(8,128)(2,1)S(1)} %get-tuple-element.80.refs_0_, bf16[2,128,1024]{2,1,0:T(8,128)(2,1)S(1)} %get-tuple-element.86.refs_1_, ...), custom_call_target="tpu_custom_call" | custom-call | flops 2000000000 | bytes 1048576 | tf_op jit(solution)/shard_map/join_halves/pallas_call | solution.py:99
  (2 shorter events, 0.0 us)
Async XLA Ops:
  0.6 9.1 %copy-start.4 = (s32[32,12]{0,1:T(8,128)S(1)}, s32[32,12]{0,1:T(8,128)}, u32[]{:S(2)}) copy-start(s32[32,12]{0,1:T(8,128)} %param.12) | copy-start | bytes 4612
  4.2 1.7 %collective-permute-start = (bf16[2,2,128,128]{3,2,1,0:T(8,128)(2,1)S(1)}, bf16[2,2,128,128]{3,2,1,0:T(8,128)(2,1)S(1)}, u32[]{:S(2)}, u32[]{:S(2)}) collective-permute-start(bf16[2,2,128,128]{3,2,1,0:T(8,128)(2,1)S(1)} %get-tuple-element.52), channel_id=1, source_target_pairs={{0,1},{1,0},{2,3},{3,2},{4,5},{5,4},{6,7},{7,6},{8,9},{9,8},{10,11... | collective-permute-start | bytes 393224 | tf_op jit(solution)/shard_map/ppermute | solution.py:506
  5.9 20.6 %collective-permute-start.4 = (bf16[2,2,8,128,128]{4,3,2,1,0:T(8,128)(2,1)S(1)}, bf16[2,2,8,128,128]{4,3,2,1,0:T(8,128)(2,1)S(1)}, u32[]{:S(2)}, u32[]{:S(2)}) collective-permute-start(bf16[2,2,8,128,128]{4,3,2,1,0:T(8,128)(2,1)S(1)} %get-tuple-element.60), channel_id=1, source_target_pairs={{0,1},{1,0},{2,3},{3,2},{4,5},{5,4},{6,7},{7,6},{8,9},{9,8},{10,11... | collective-permute-start | bytes 3145736 | tf_op jit(solution)/shard_map/ppermute | solution.py:506
  6.3 9.6 %collective-permute-start.3 = (bf16[2,2,2,128,128]{4,3,2,1,0:T(8,128)(2,1)S(1)}, bf16[2,2,2,128,128]{4,3,2,1,0:T(8,128)(2,1)S(1)}, u32[]{:S(2)}, u32[]{:S(2)}) collective-permute-start(bf16[2,2,2,128,128]{4,3,2,1,0:T(8,128)(2,1)S(1)} %pad_maximum_fusion.rest_0_.rest_7_), channel_id=1, source_target_pairs={{0,8},{8,16},{16,24},{1,9},{9,17},{17,25},{2,10},{10,18},{18,26},{... | collective-permute-start | bytes 786440 | tf_op jit(solution)/shard_map/ppermute | solution.py:512
  9.4 11.9 %collective-permute-start.2 = (bf16[2,2,2,128,128]{4,3,2,1,0:T(8,128)(2,1)S(1)}, bf16[2,2,2,128,128]{4,3,2,1,0:T(8,128)(2,1)S(1)}, u32[]{:S(2)}, u32[]{:S(2)}) collective-permute-start(bf16[2,2,2,128,128]{4,3,2,1,0:T(8,128)(2,1)S(1)} %pad_maximum_fusion.rest_0_.rest_7_), channel_id=1, source_target_pairs={{0,2},{1,3},{2,0},{3,1},{4,6},{5,7},{6,4},{7,5},{8,10},{9,11},{10,... | collective-permute-start | bytes 786440 | tf_op jit(solution)/shard_map/ppermute | solution.py:506
  9.7 13.7 %collective-permute-start.1 = (bf16[2,2,2,128,128]{4,3,2,1,0:T(8,128)(2,1)S(1)}, bf16[2,2,2,128,128]{4,3,2,1,0:T(8,128)(2,1)S(1)}, u32[]{:S(2)}, u32[]{:S(2)}) collective-permute-start(bf16[2,2,2,128,128]{4,3,2,1,0:T(8,128)(2,1)S(1)} %pad_maximum_fusion.rest_0_.rest_7_), channel_id=1, source_target_pairs={{0,4},{1,5},{2,6},{3,7},{4,0},{5,1},{6,2},{7,3},{8,12},{9,13},{10,... | collective-permute-start | bytes 786440 | tf_op jit(solution)/shard_map/ppermute | solution.py:506
  12.5 0.6 copy-start.2
  13.1 13.5 %copy-start.3 = (s32[2,4]{1,0:T(2,128)}, s32[2,4]{1,0:T(2,128)S(1)}, u32[]{:S(2)}) copy-start(s32[2,4]{1,0:T(2,128)S(1)} %get-tuple-element.58.counts) | copy-start | bytes 100
  13.1 23.7 %copy-start.1 = (bf16[2,2,8,128,128]{4,3,2,1,0:T(8,128)(2,1)S(1)}, bf16[2,2,8,128,128]{4,3,2,1,0:T(8,128)(2,1)}, u32[]{:S(2)}) copy-start(bf16[2,2,8,128,128]{4,3,2,1,0:T(8,128)(2,1)} %get-tuple-element.59.own) | copy-start | bytes 3145732
  23.4 13.4 %collective-permute-start.6 = (bf16[2,2,2,128,128]{4,3,2,1,0:T(8,128)(2,1)S(1)}, bf16[2,2,2,128,128]{4,3,2,1,0:T(8,128)(2,1)S(1)}, u32[]{:S(2)}, u32[]{:S(2)}) collective-permute-start(bf16[2,2,2,128,128]{4,3,2,1,0:T(8,128)(2,1)S(1)} %collective-permute-done.1.rest_1_.rest_0_.rest_9_), channel_id=1, source_target_pairs={{0,2},{1,3},{2,0},{3,1},{4,6},{5,7},{6,4},{7,5},{8,10},{9,11},{10,... | collective-permute-start | bytes 786440 | tf_op jit(solution)/shard_map/ppermute | solution.py:506
  23.4 8.1 %collective-permute-start.5 = (bf16[2,2,2,128,128]{4,3,2,1,0:T(8,128)(2,1)S(1)}, bf16[2,2,2,128,128]{4,3,2,1,0:T(8,128)(2,1)S(1)}, u32[]{:S(2)}, u32[]{:S(2)}) collective-permute-start(bf16[2,2,2,128,128]{4,3,2,1,0:T(8,128)(2,1)S(1)} %collective-permute-done.1.rest_1_.rest_0_.rest_9_), channel_id=1, source_target_pairs={{0,8},{8,16},{16,24},{1,9},{9,17},{17,25},{2,10},{10,18},{18,26},{... | collective-permute-start | bytes 786440 | tf_op jit(solution)/shard_map/ppermute | solution.py:512
  31.5 8.2 %collective-permute-start.7 = (bf16[2,2,2,128,128]{4,3,2,1,0:T(8,128)(2,1)S(1)}, bf16[2,2,2,128,128]{4,3,2,1,0:T(8,128)(2,1)S(1)}, u32[]{:S(2)}, u32[]{:S(2)}) collective-permute-start(bf16[2,2,2,128,128]{4,3,2,1,0:T(8,128)(2,1)S(1)} %collective-permute-done.2.rest_1_.rest_8_), channel_id=1, source_target_pairs={{0,8},{8,16},{16,24},{1,9},{9,17},{17,25},{2,10},{10,18},{18,26},{... | collective-permute-start | bytes 786440 | tf_op jit(solution)/shard_map/ppermute | solution.py:512
  35.5 5.6 %collective-permute-start.8 = (bf16[2,2,2,128,128]{4,3,2,1,0:T(8,128)(2,1)S(1)}, bf16[2,2,2,128,128]{4,3,2,1,0:T(8,128)(2,1)S(1)}, u32[]{:S(2)}, u32[]{:S(2)}) collective-permute-start(bf16[2,2,2,128,128]{4,3,2,1,0:T(8,128)(2,1)S(1)} %collective-permute-done.5.rest_2_.rest_5_), channel_id=1, source_target_pairs={{0,2},{1,3},{2,0},{3,1},{4,6},{5,7},{6,4},{7,5},{8,10},{9,11},{10,... | collective-permute-start | bytes 786440 | tf_op jit(solution)/shard_map/ppermute | solution.py:506
  50.8 11.2 %collective-permute-start.9 = (bf16[2,2,2,128,128]{4,3,2,1,0:T(8,128)(2,1)S(1)}, bf16[2,2,2,128,128]{4,3,2,1,0:T(8,128)(2,1)S(1)}, u32[]{:S(2)}, u32[]{:S(2)}) collective-permute-start(bf16[2,2,2,128,128]{4,3,2,1,0:T(8,128)(2,1)S(1)} %get-tuple-element.66), channel_id=1, source_target_pairs={{0,2},{1,3},{2,0},{3,1},{4,6},{5,7},{6,4},{7,5},{8,10},{9,11},{10,... | collective-permute-start | bytes 786440 | tf_op jit(solution)/shard_map/ppermute | solution.py:506
  55.0 23.7 %collective-permute-start.12 = (bf16[4,2,2,128,128]{4,3,2,1,0:T(8,128)(2,1)S(1)}, bf16[4,2,2,128,128]{4,3,2,1,0:T(8,128)(2,1)S(1)}, u32[]{:S(2)}, u32[]{:S(2)}) collective-permute-start(bf16[4,2,2,128,128]{4,3,2,1,0:T(8,128)(2,1)S(1)} %get-tuple-element.83), channel_id=1, source_target_pairs={{8,0},{16,8},{24,16},{9,1},{17,9},{25,17},{10,2},{18,10},{26,18},{... | collective-permute-start | bytes 1572872 | tf_op jit(solution)/shard_map/ppermute | solution.py:515
  62.1 17.0 %copy-start = (f32[320,128]{1,0:T(8,128)S(1)}, f32[320,128]{1,0:T(8,128)}, u32[]{:S(2)}) copy-start(f32[320,128]{1,0:T(8,128)} %constant.2.clone.refs_4_.rest_11_.rest_4_) | copy-start | bytes 491524
  62.1 11.3 %collective-permute-start.10 = (bf16[2,2,2,128,128]{4,3,2,1,0:T(8,128)(2,1)S(1)}, bf16[2,2,2,128,128]{4,3,2,1,0:T(8,128)(2,1)S(1)}, u32[]{:S(2)}, u32[]{:S(2)}) collective-permute-start(bf16[2,2,2,128,128]{4,3,2,1,0:T(8,128)(2,1)S(1)} %add_convert_fusion.2), channel_id=1, source_target_pairs={{8,0},{16,8},{24,16},{9,1},{17,9},{25,17},{10,2},{18,10},{26,18},{... | collective-permute-start | bytes 786440 | tf_op jit(solution)/shard_map/ppermute | solution.py:515
  64.1 9.3 %collective-permute-start.11 = (bf16[2,2,2,128,128]{4,3,2,1,0:T(8,128)(2,1)S(1)}, bf16[2,2,2,128,128]{4,3,2,1,0:T(8,128)(2,1)S(1)}, u32[]{:S(2)}, u32[]{:S(2)}) collective-permute-start(bf16[2,2,2,128,128]{4,3,2,1,0:T(8,128)(2,1)S(1)} %get-tuple-element.74), channel_id=1, source_target_pairs={{0,2},{1,3},{2,0},{3,1},{4,6},{5,7},{6,4},{7,5},{8,10},{9,11},{10,... | collective-permute-start | bytes 786440 | tf_op jit(solution)/shard_map/ppermute | solution.py:506
  73.5 20.9 %collective-permute-start.16 = (bf16[2,2,2,128,128]{4,3,2,1,0:T(8,128)(2,1)S(1)}, bf16[2,2,2,128,128]{4,3,2,1,0:T(8,128)(2,1)S(1)}, u32[]{:S(2)}, u32[]{:S(2)}) collective-permute-start(bf16[2,2,2,128,128]{4,3,2,1,0:T(8,128)(2,1)S(1)} %add_convert_fusion.1), channel_id=1, source_target_pairs={{0,4},{1,5},{2,6},{3,7},{4,0},{5,1},{6,2},{7,3},{8,12},{9,13},{10,... | collective-permute-start | bytes 786440 | tf_op jit(solution)/shard_map/ppermute | solution.py:506
  78.7 15.6 %collective-permute-start.15 = (bf16[2,2,2,128,128]{4,3,2,1,0:T(8,128)(2,1)S(1)}, bf16[2,2,2,128,128]{4,3,2,1,0:T(8,128)(2,1)S(1)}, u32[]{:S(2)}, u32[]{:S(2)}) collective-permute-start(bf16[2,2,2,128,128]{4,3,2,1,0:T(8,128)(2,1)S(1)} %add_convert_fusion), channel_id=1, source_target_pairs={{0,2},{1,3},{2,0},{3,1},{4,6},{5,7},{6,4},{7,5},{8,10},{9,11},{10,... | collective-permute-start | bytes 786440 | tf_op jit(solution)/shard_map/ppermute | solution.py:506
  89.2 7.6 %collective-permute-start.13 = (bf16[2,128,1024]{2,1,0:T(8,128)(2,1)S(1)}, bf16[2,128,1024]{2,1,0:T(8,128)(2,1)S(1)}, u32[]{:S(2)}, u32[]{:S(2)}) collective-permute-start(bf16[2,128,1024]{2,1,0:T(8,128)(2,1)S(1)} %get-tuple-element.89), channel_id=1, source_target_pairs={{0,1},{1,0},{2,3},{3,2},{4,5},{5,4},{6,7},{7,6},{8,9},{9,8},{10,11... | collective-permute-start | bytes 1572872 | tf_op jit(solution)/shard_map/ppermute | solution.py:506
  94.3 2.5 %collective-permute-start.14 = (bf16[2,128,1024]{2,1,0:T(8,128)(2,1)S(1)}, bf16[2,128,1024]{2,1,0:T(8,128)(2,1)S(1)}, u32[]{:S(2)}, u32[]{:S(2)}) collective-permute-start(bf16[2,128,1024]{2,1,0:T(8,128)(2,1)S(1)} %get-tuple-element.90), channel_id=1, source_target_pairs={{0,1},{1,0},{2,3},{3,2},{4,5},{5,4},{6,7},{7,6},{8,9},{9,8},{10,11... | collective-permute-start | bytes 1572872 | tf_op jit(solution)/shard_map/ppermute | solution.py:506
  95.2 1.5 %collective-permute-start.17 = (bf16[2,128,256]{2,1,0:T(8,128)(2,1)S(1)}, bf16[2,128,256]{2,1,0:T(8,128)(2,1)S(1)}, u32[]{:S(2)}, u32[]{:S(2)}) collective-permute-start(bf16[2,128,256]{2,1,0:T(8,128)(2,1)S(1)} %get-tuple-element.95), channel_id=1, source_target_pairs={{0,1},{1,0},{2,3},{3,2},{4,5},{5,4},{6,7},{7,6},{8,9},{9,8},{10,11... | collective-permute-start | bytes 393224 | tf_op jit(solution)/shard_map/ppermute | solution.py:506

commit v3 on v0

--- a/solution.py
+++ b/solution.py
@@ -433,15 +433,18 @@
         total = stops[-1]
         result = outs[i * HALF_KV + h]
 
-        @pl.when(lax.rem(total, 2) == 1)
-        def _():
-            low[h, i, total] = jnp.zeros((2, BLK, ROWS), BF16)
+        filled = lax.div(total + 3, 4) * 4
+        for extra in range(3):
+
+            @pl.when(total + extra < filled)
+            def _():
+                low[h, i, total + extra] = jnp.zeros((2, BLK, ROWS), BF16)
 
         out_acc[...] = jnp.zeros_like(out_acc)
         dq_acc[...] = jnp.zeros_like(dq_acc)
 
         def add(n, _):
-            pair = (2 * n, 2 * n + 1)
+            pair = [4 * n + m for m in range(4)]
             for m in pair:
                 for source, first, stop in zip(saved, stops, stops[1:]):
 
@@ -449,7 +452,7 @@
                     def _():
                         copy(source, h, i, m, first).wait()
 
-            found = [lists[i, 3, m] for m in pair]
+            found = [jnp.where(m < total, lists[i, 3, jnp.minimum(m, total)], 0) for m in pair]
             keys_t = jnp.concatenate([store[e, 0, h].T for e in found], axis=1)
             values_t = jnp.concatenate([store[e, 1, h].T for e in found], axis=1)
             for _, columns in chunks():
@@ -459,7 +462,7 @@
                 dq_acc[:, columns] += dot_nn(keys_t, dscores)
             return 0
 
-        lax.fori_loop(0, lax.div(total + 1, 2), add, 0)
+        lax.fori_loop(0, lax.div(filled, 4), add, 0)
         cosine, sine = tables[i]
         for r in range(RATIO):
             rows = slice(r * BLK, (r + 1) * BLK)
@@ -622,7 +625,7 @@
     half_out = jax.ShapeDtypeStruct((2, BLK, RATIO * HEAD_DIM), BF16)
     place_late, _ = lax.optimization_barrier((block_position, merged))
     wide = pltpu.VMEM((HEAD_DIM, ROWS), F32)
-    slots = (HALF_KV, 2, n_listed + 1)
+    slots = (HALF_KV, 2, n_listed + 3)
     halves = call(
         functools.partial(query_results, n_seq), (half_out,) * (2 * HALF_KV), 3,
         [

time: 97.4 us -> 96.5 us (level)
  the two profiles are of different devices: /device:TPU:5 before, /device:TPU:31 now
where the time goes in v3:
time: 96.5 us; the launch traced here: 96.1 us
  Pallas kernels  38.9 us (40%)
  starting transfers between devices  33.3 us (35%)
  waiting for transfers between devices  21.5 us (22%)
  local copies, waits for them, and re-layouts  1.31 us (1%)
    pallas_call x10, Pallas kernels, run(): pl.pallas_call(kernel, out_shape=[placed(n, a) for n, a in enumerate(outs...  38.9 us
    ppermute x13, starting transfers between devices, cross(): return lax.ppermute(array, 'seq', [(m, m ^ by) for m in range(n_seq)])  21.2 us
    ppermute x3, waiting for transfers between devices, onward(): return lax.ppermute(array, 'grp', [(g, g + 1) for g in range(n_grp - 1)])  12 us
    ppermute x2, starting transfers between devices, back(): return lax.ppermute(array, 'grp', [(g + 1, g) for g in range(n_grp - 1)])  8.17 us
    ppermute x13, waiting for transfers between devices, cross(): return lax.ppermute(array, 'seq', [(m, m ^ by) for m in range(n_seq)])  7.88 us
    ppermute x3, starting transfers between devices, onward(): return lax.ppermute(array, 'grp', [(g, g + 1) for g in range(n_grp - 1)])  3.85 us
  transfers between devices with their start and end apart: 18, of which 8 were waited for; matrix products, arithmetic and copies ran while one was open for 1% of the time, Pallas kernels for 27%

profile of v3, /device:TPU:31, one launch (start us, length us, event | category | flops | bytes accessed | tf_op | source)
XLA Modules:
  0.0 96.1 jit_solution(15408005118871258637)
XLA Ops:
  0.6 0.0 copy-start.4
  0.6 3.5 %prepare.1 = (bf16[2,2,128,128]{3,2,1,0:T(8,128)(2,1)S(1)}, bf16[2,2,128,128]{3,2,1,0:T(8,128)(2,1)S(1)}, bf16[2,2,8,128,128]{4,3,2,1,0:T(8,128)(2,1)}, bf16[2,2,8,128,128]{4,3,2,1,0:T(8,128)(2,1)S(1)}) custom-call(s32[32]{0:T(128)} %place_ref.4, bf16[128,512]{1,0:T(8,128)(2,1)} %refs_0_.1, bf16[128,512]{1,0:T(8,128)(2,1)} %refs_1_.1, ...), custom_call_target="tpu_custom_call" | custom-call | flops 3000000000 | bytes 1048576 | tf_op jit(solution)/shard_map/prepare/pallas_call | solution.py:99
  4.2 0.7 collective-permute-start
  4.9 1.0 %collective-permute-done = bf16[2,2,128,128]{3,2,1,0:T(8,128)(2,1)S(1)} collective-permute-done((bf16[2,2,128,128]{3,2,1,0:T(8,128)(2,1)S(1)}, bf16[2,2,128,128]{3,2,1,0:T(8,128)(2,1)S(1)}, u32[]{:S(2)}, u32[]{:S(2)}) %collective-permute-start) | collective-permute-done | bytes 131104 | tf_op jit(solution)/shard_map/ppermute | solution.py:510
  5.9 0.4 collective-permute-start.4
  6.3 1.3 %collective-permute-start.3 = (bf16[2,2,2,128,128]{4,3,2,1,0:T(8,128)(2,1)S(1)}, bf16[2,2,2,128,128]{4,3,2,1,0:T(8,128)(2,1)S(1)}, u32[]{:S(2)}, u32[]{:S(2)}) collective-permute-start(bf16[2,2,2,128,128]{4,3,2,1,0:T(8,128)(2,1)S(1)} %pad_maximum_fusion.rest_0_.rest_7_), channel_id=1, source_target_pairs={{0,8},{8,16},{16,24},{1,9},{9,17},{17,25},{2,10},{10,18},{18,26},{... | collective-permute-start | bytes 786440 | tf_op jit(solution)/shard_map/ppermute | solution.py:516
  7.6 0.2 collective-permute-start.2
  7.8 0.1 collective-permute-start.1
  7.9 0.0 copy-done.4
  7.9 0.7 copy.12.key_blocks
  8.6 1.9 %block_lists.1 = (s32[2,4,13]{2,1,0:T(4,128)S(1)}, s32[2,4]{1,0:T(2,128)S(1)}) custom-call(s32[32,12]{1,0:T(8,128)} %copy.12.key_blocks, s32[32]{0:T(128)} %key_counts.1), custom_call_target="tpu_custom_call" | custom-call | flops 2000000000 | bytes 1048576 | tf_op jit(solution)/shard_map/block_lists/pallas_call | solution.py:99
  10.5 0.0 copy-start.2
  10.6 0.6 copy-done.2
  11.1 0.0 copy-start.3
  11.1 0.0 copy-start.1
  11.1 4.8 %collective-permute-done.3.rest_0_.rest_3_ = bf16[2,2,2,128,128]{4,3,2,1,0:T(8,128)(2,1)S(1)} collective-permute-done((bf16[2,2,2,128,128]{4,3,2,1,0:T(8,128)(2,1)S(1)}, bf16[2,2,2,128,128]{4,3,2,1,0:T(8,128)(2,1)S(1)}, u32[]{:S(2)}, u32[]{:S(2)}) %collective-permute-start.3) | collective-permute-done | bytes 262176 | tf_op jit(solution)/shard_map/ppermute | solution.py:516
  16.0 3.8 %collective-permute-done.2.rest_1_.rest_8_ = bf16[2,2,2,128,128]{4,3,2,1,0:T(8,128)(2,1)S(1)} collective-permute-done((bf16[2,2,2,128,128]{4,3,2,1,0:T(8,128)(2,1)S(1)}, bf16[2,2,2,128,128]{4,3,2,1,0:T(8,128)(2,1)S(1)}, u32[]{:S(2)}, u32[]{:S(2)}) %collective-permute-start.2) | collective-permute-done | bytes 262176 | tf_op jit(solution)/shard_map/ppermute | solution.py:510
  19.8 2.0 %collective-permute-done.1.rest_1_.rest_0_.rest_9_ = bf16[2,2,2,128,128]{4,3,2,1,0:T(8,128)(2,1)S(1)} collective-permute-done((bf16[2,2,2,128,128]{4,3,2,1,0:T(8,128)(2,1)S(1)}, bf16[2,2,2,128,128]{4,3,2,1,0:T(8,128)(2,1)S(1)}, u32[]{:S(2)}, u32[]{:S(2)}) %collective-permute-start.1) | collective-permute-done | bytes 262176 | tf_op jit(solution)/shard_map/ppermute | solution.py:510
  21.8 0.0 collective-permute-start.6
  21.9 1.3 %collective-permute-start.5 = (bf16[2,2,2,128,128]{4,3,2,1,0:T(8,128)(2,1)S(1)}, bf16[2,2,2,128,128]{4,3,2,1,0:T(8,128)(2,1)S(1)}, u32[]{:S(2)}, u32[]{:S(2)}) collective-permute-start(bf16[2,2,2,128,128]{4,3,2,1,0:T(8,128)(2,1)S(1)} %collective-permute-done.1.rest_1_.rest_0_.rest_9_), channel_id=1, source_target_pairs={{0,8},{8,16},{16,24},{1,9},{9,17},{17,25},{2,10},{10,18},{18,26},{... | collective-permute-start | bytes 786440 | tf_op jit(solution)/shard_map/ppermute | solution.py:516
  23.1 0.0 collective-permute-done.4.other
  23.2 0.0 copy-done.3
  23.2 2.9 %near_statistics.1.rest_0_ = f32[2,2,8,1024]{3,2,1,0:T(8,128)S(1)} custom-call(s32[2,4,13]{2,1,0:T(4,128)} %copy-done.2, s32[2,4]{1,0:T(2,128)} %copy-done.3, bf16[2,2,8,128,128]{4,3,2,1,0:T(8,128)(2,1)} %get-tuple-element.59.own, bf16[2,2,8,128,128]{4,3,2,1,0:T(8,128)(2,1)S(1)} %collective-permute-done.4.other, ...), custom_call_target="tpu_custom_call" | custom-call | flops 4000000000 | bytes 1048576 | tf_op jit(solution)/shard_map/near_statistics/pallas_call | solution.py:99
  26.0 4.6 %collective-permute-done.5.rest_2_.rest_5_ = bf16[2,2,2,128,128]{4,3,2,1,0:T(8,128)(2,1)S(1)} collective-permute-done((bf16[2,2,2,128,128]{4,3,2,1,0:T(8,128)(2,1)S(1)}, bf16[2,2,2,128,128]{4,3,2,1,0:T(8,128)(2,1)S(1)}, u32[]{:S(2)}, u32[]{:S(2)}) %collective-permute-start.5) | collective-permute-done | bytes 262176 | tf_op jit(solution)/shard_map/ppermute | solution.py:516
  30.6 1.3 %collective-permute-start.7 = (bf16[2,2,2,128,128]{4,3,2,1,0:T(8,128)(2,1)S(1)}, bf16[2,2,2,128,128]{4,3,2,1,0:T(8,128)(2,1)S(1)}, u32[]{:S(2)}, u32[]{:S(2)}) collective-permute-start(bf16[2,2,2,128,128]{4,3,2,1,0:T(8,128)(2,1)S(1)} %collective-permute-done.2.rest_1_.rest_8_), channel_id=1, source_target_pairs={{0,8},{8,16},{16,24},{1,9},{9,17},{17,25},{2,10},{10,18},{18,26},{... | collective-permute-start | bytes 786440 | tf_op jit(solution)/shard_map/ppermute | solution.py:516
  31.9 1.2 %collective-permute-start.8 = (bf16[2,2,2,128,128]{4,3,2,1,0:T(8,128)(2,1)S(1)}, bf16[2,2,2,128,128]{4,3,2,1,0:T(8,128)(2,1)S(1)}, u32[]{:S(2)}, u32[]{:S(2)}) collective-permute-start(bf16[2,2,2,128,128]{4,3,2,1,0:T(8,128)(2,1)S(1)} %collective-permute-done.5.rest_2_.rest_5_), channel_id=1, source_target_pairs={{0,2},{1,3},{2,0},{3,1},{4,6},{5,7},{6,4},{7,5},{8,10},{9,11},{10,... | collective-permute-start | bytes 786440 | tf_op jit(solution)/shard_map/ppermute | solution.py:510
  33.1 0.0 collective-permute-done.6.rest_2_.rest_1_.rest_10_
  33.1 0.0 copy-done.1
  33.2 2.9 %far_statistics.1.stats_in = f32[2,2,8,1024]{3,2,1,0:T(8,128)S(1)} custom-call(s32[2,4,13]{2,1,0:T(4,128)} %copy-done.2, s32[2,4]{1,0:T(2,128)} %copy-done.3, bf16[2,2,8,128,128]{4,3,2,1,0:T(8,128)(2,1)S(1)} %copy-done.1, bf16[2,2,8,128,128]{4,3,2,1,0:T(8,128)(2,1)S(1)} %collective-permute-done.4.other, f32[2,2,8,1024]{3,2,1,0:T(8,128)S(1)} %near_statistics.1.rest_0_, ...), custom_call_target="tpu_custom_call" | custom-call | flops 4000000000 | bytes 1048576 | tf_op jit(solution)/shard_map/far_statistics/pallas_call | solution.py:99
  36.1 2.6 %collective-permute-done.7.rest_1_.rest_4_ = bf16[2,2,2,128,128]{4,3,2,1,0:T(8,128)(2,1)S(1)} collective-permute-done((bf16[2,2,2,128,128]{4,3,2,1,0:T(8,128)(2,1)S(1)}, bf16[2,2,2,128,128]{4,3,2,1,0:T(8,128)(2,1)S(1)}, u32[]{:S(2)}, u32[]{:S(2)}) %collective-permute-start.7) | collective-permute-done | bytes 262176 | tf_op jit(solution)/shard_map/ppermute | solution.py:516
  38.7 0.0 collective-permute-done.8.rest_3_.rest_6_
  38.7 7.9 %previous_gradients.1 = (bf16[4,2,2,128,128]{4,3,2,1,0:T(8,128)(2,1)S(1)}, bf16[2,2,2,128,128]{4,3,2,1,0:T(8,128)(2,1)S(1)}, bf16[2,2,2,128,128]{4,3,2,1,0:T(8,1...) custom-call(s32[2,4,13]{2,1,0:T(4,128)} %copy-done.2, s32[2,4]{1,0:T(2,128)} %copy-done.3, ...), custom_call_target="tpu_custom_call" | custom-call | flops 14000000000 | bytes 1048576 | tf_op jit(solution)/shard_map/previous_gradients/pallas_call | solution.py:99
  46.6 1.1 %collective-permute-start.9 = (bf16[2,2,2,128,128]{4,3,2,1,0:T(8,128)(2,1)S(1)}, bf16[2,2,2,128,128]{4,3,2,1,0:T(8,128)(2,1)S(1)}, u32[]{:S(2)}, u32[]{:S(2)}) collective-permute-start(bf16[2,2,2,128,128]{4,3,2,1,0:T(8,128)(2,1)S(1)} %get-tuple-element.66), channel_id=1, source_target_pairs={{0,2},{1,3},{2,0},{3,1},{4,6},{5,7},{6,4},{7,5},{8,10},{9,11},{10,... | collective-permute-start | bytes 786440 | tf_op jit(solution)/shard_map/ppermute | solution.py:510
  47.7 4.0 %collective-permute-start.12 = (bf16[4,2,2,128,128]{4,3,2,1,0:T(8,128)(2,1)S(1)}, bf16[4,2,2,128,128]{4,3,2,1,0:T(8,128)(2,1)S(1)}, u32[]{:S(2)}, u32[]{:S(2)}) collective-permute-start(bf16[4,2,2,128,128]{4,3,2,1,0:T(8,128)(2,1)S(1)} %get-tuple-element.83), channel_id=1, source_target_pairs={{8,0},{16,8},{24,16},{9,1},{17,9},{25,17},{10,2},{18,10},{26,18},{... | collective-permute-start | bytes 1572872 | tf_op jit(solution)/shard_map/ppermute | solution.py:519
  51.7 4.5 %far_current_gradients.1 = (f32[2,2,2,128,128]{4,3,2,1,0:T(8,128)S(1)}, bf16[2,2,2,128,128]{4,3,2,1,0:T(8,128)(2,1)S(1)}, bf16[2,4,2,2,128,1024]{5,4,3,2,1,0:T(8,128)(2,1)}) custom-call(s32[2,4,13]{2,1,0:T(4,128)} %copy-done.2, s32[2,4]{1,0:T(2,128)} %copy-done.3, bf16[2,2,8,128,128]{4,3,2,1,0:T(8,128)(2,1)S(1)} %copy-done.1, ...), custom_call_target="tpu_custom_call" | custom-call | flops 6000000000 | bytes 1048576 | tf_op jit(solution)/shard_map/far_current_gradients/pallas_call | solution.py:99
  56.2 0.0 collective-permute-done.9
  56.2 0.1 add_convert_fusion.2
  56.3 0.0 copy-start
  56.3 4.2 %collective-permute-start.10 = (bf16[2,2,2,128,128]{4,3,2,1,0:T(8,128)(2,1)S(1)}, bf16[2,2,2,128,128]{4,3,2,1,0:T(8,128)(2,1)S(1)}, u32[]{:S(2)}, u32[]{:S(2)}) collective-permute-start(bf16[2,2,2,128,128]{4,3,2,1,0:T(8,128)(2,1)S(1)} %add_convert_fusion.2), channel_id=1, source_target_pairs={{8,0},{16,8},{24,16},{9,1},{17,9},{25,17},{10,2},{18,10},{26,18},{... | collective-permute-start | bytes 786440 | tf_op jit(solution)/shard_map/ppermute | solution.py:519
  60.5 0.1 collective-permute-start.11
  60.6 4.2 %near_current_gradients.1 = (f32[2,2,2,128,128]{4,3,2,1,0:T(8,128)S(1)}, f32[2,2,2,128,128]{4,3,2,1,0:T(8,128)S(1)}, bf16[2,4,2,2,128,1024]{5,4,3,2,1,0:T(8,128)(2,1)}) custom-call(s32[2,4,13]{2,1,0:T(4,128)} %copy-done.2, s32[2,4]{1,0:T(2,128)} %copy-done.3, bf16[2,2,8,128,128]{4,3,2,1,0:T(8,128)(2,1)S(1)} %copy-done.1, ...), custom_call_target="tpu_custom_call" | custom-call | flops 6000000000 | bytes 1048576 | tf_op jit(solution)/shard_map/near_current_gradients/pallas_call | solution.py:99
  64.9 1.6 %collective-permute-done.10 = bf16[2,2,2,128,128]{4,3,2,1,0:T(8,128)(2,1)S(1)} collective-permute-done((bf16[2,2,2,128,128]{4,3,2,1,0:T(8,128)(2,1)S(1)}, bf16[2,2,2,128,128]{4,3,2,1,0:T(8,128)(2,1)S(1)}, u32[]{:S(2)}, u32[]{:S(2)}) %collective-permute-start.10) | collective-permute-done | bytes 262176 | tf_op jit(solution)/shard_map/ppermute | solution.py:519
  66.5 0.0 collective-permute-done.11
  66.5 0.1 add_convert_fusion.1
  66.6 4.8 %collective-permute-start.16 = (bf16[2,2,2,128,128]{4,3,2,1,0:T(8,128)(2,1)S(1)}, bf16[2,2,2,128,128]{4,3,2,1,0:T(8,128)(2,1)S(1)}, u32[]{:S(2)}, u32[]{:S(2)}) collective-permute-start(bf16[2,2,2,128,128]{4,3,2,1,0:T(8,128)(2,1)S(1)} %add_convert_fusion.1), channel_id=1, source_target_pairs={{0,4},{1,5},{2,6},{3,7},{4,0},{5,1},{6,2},{7,3},{8,12},{9,13},{10,... | collective-permute-start | bytes 786440 | tf_op jit(solution)/shard_map/ppermute | solution.py:510
  71.4 0.0 collective-permute-done.12
  71.4 0.1 add_convert_fusion
  71.4 1.2 %collective-permute-start.15 = (bf16[2,2,2,128,128]{4,3,2,1,0:T(8,128)(2,1)S(1)}, bf16[2,2,2,128,128]{4,3,2,1,0:T(8,128)(2,1)S(1)}, u32[]{:S(2)}, u32[]{:S(2)}) collective-permute-start(bf16[2,2,2,128,128]{4,3,2,1,0:T(8,128)(2,1)S(1)} %add_convert_fusion), channel_id=1, source_target_pairs={{0,2},{1,3},{2,0},{3,1},{4,6},{5,7},{6,4},{7,5},{8,10},{9,11},{10,... | collective-permute-start | bytes 786440 | tf_op jit(solution)/shard_map/ppermute | solution.py:510
  72.7 0.0 copy-done
  72.7 8.6 %query_results.1 = (bf16[2,128,1024]{2,1,0:T(8,128)(2,1)S(1)}, bf16[2,128,1024]{2,1,0:T(8,128)(2,1)S(1)}, bf16[2,128,1024]{2,1,0:T(8,128)(2,1)S(1)}, bf16[2,128,1024]{2,1,0:T(8,128)(2,1)S(1)}) custom-call(s32[2,4,13]{2,1,0:T(4,128)} %copy-done.2, s32[2,4]{1,0:T(2,128)} %copy-done.3, s32[32]{0:T(128)} %place_ref.4, ...), custom_call_target="tpu_custom_call" | custom-call | flops 20000000000 | bytes 1048576 | tf_op jit(solution)/shard_map/query_results/pallas_call | solution.py:99
  81.2 10.8 %collective-permute-start.13 = (bf16[2,128,1024]{2,1,0:T(8,128)(2,1)S(1)}, bf16[2,128,1024]{2,1,0:T(8,128)(2,1)S(1)}, u32[]{:S(2)}, u32[]{:S(2)}) collective-permute-start(bf16[2,128,1024]{2,1,0:T(8,128)(2,1)S(1)} %get-tuple-element.89), channel_id=1, source_target_pairs={{0,1},{1,0},{2,3},{3,2},{4,5},{5,4},{6,7},{7,6},{8,9},{9,8},{10,11... | collective-permute-start | bytes 1572872 | tf_op jit(solution)/shard_map/ppermute | solution.py:510
  92.0 0.1 collective-permute-start.14
  92.1 0.0 collective-permute-done.16.rest_3_
  92.1 0.0 collective-permute-done.15.rest_2_
  92.1 0.9 key_gradients.1
  93.0 0.5 collective-permute-start.17
  93.5 1.0 %collective-permute-done.17.refs_5_ = bf16[2,128,256]{2,1,0:T(8,128)(2,1)S(1)} collective-permute-done((bf16[2,128,256]{2,1,0:T(8,128)(2,1)S(1)}, bf16[2,128,256]{2,1,0:T(8,128)(2,1)S(1)}, u32[]{:S(2)}, u32[]{:S(2)}) %collective-permute-start.17) | collective-permute-done | bytes 131104 | tf_op jit(solution)/shard_map/ppermute | solution.py:510
  94.5 0.0 collective-permute-done.13.refs_2_
  94.5 0.0 collective-permute-done.14.refs_3_
  94.5 1.6 %join_halves.1 = (bf16[128,4096]{1,0:T(8,128)(2,1)}, bf16[128,4096]{1,0:T(8,128)(2,1)}, bf16[128,512]{1,0:T(8,128)(2,1)}, bf16[128,512]{1,0:T(8,128)(2,1)}) custom-call(bf16[2,128,1024]{2,1,0:T(8,128)(2,1)S(1)} %get-tuple-element.80.refs_0_, bf16[2,128,1024]{2,1,0:T(8,128)(2,1)S(1)} %get-tuple-element.86.refs_1_, ...), custom_call_target="tpu_custom_call" | custom-call | flops 2000000000 | bytes 1048576 | tf_op jit(solution)/shard_map/join_halves/pallas_call | solution.py:99
  (2 shorter events, 0.0 us)
Async XLA Ops:
  0.6 7.3 %copy-start.4 = (s32[32,12]{0,1:T(8,128)S(1)}, s32[32,12]{0,1:T(8,128)}, u32[]{:S(2)}) copy-start(s32[32,12]{0,1:T(8,128)} %param.12) | copy-start | bytes 4612
  4.2 1.7 %collective-permute-start = (bf16[2,2,128,128]{3,2,1,0:T(8,128)(2,1)S(1)}, bf16[2,2,128,128]{3,2,1,0:T(8,128)(2,1)S(1)}, u32[]{:S(2)}, u32[]{:S(2)}) collective-permute-start(bf16[2,2,128,128]{3,2,1,0:T(8,128)(2,1)S(1)} %get-tuple-element.52), channel_id=1, source_target_pairs={{0,1},{1,0},{2,3},{3,2},{4,5},{5,4},{6,7},{7,6},{8,9},{9,8},{10,11... | collective-permute-start | bytes 393224 | tf_op jit(solution)/shard_map/ppermute | solution.py:510
  5.9 17.2 %collective-permute-start.4 = (bf16[2,2,8,128,128]{4,3,2,1,0:T(8,128)(2,1)S(1)}, bf16[2,2,8,128,128]{4,3,2,1,0:T(8,128)(2,1)S(1)}, u32[]{:S(2)}, u32[]{:S(2)}) collective-permute-start(bf16[2,2,8,128,128]{4,3,2,1,0:T(8,128)(2,1)S(1)} %get-tuple-element.60), channel_id=1, source_target_pairs={{0,1},{1,0},{2,3},{3,2},{4,5},{5,4},{6,7},{7,6},{8,9},{9,8},{10,11... | collective-permute-start | bytes 3145736 | tf_op jit(solution)/shard_map/ppermute | solution.py:510
  6.3 9.6 %collective-permute-start.3 = (bf16[2,2,2,128,128]{4,3,2,1,0:T(8,128)(2,1)S(1)}, bf16[2,2,2,128,128]{4,3,2,1,0:T(8,128)(2,1)S(1)}, u32[]{:S(2)}, u32[]{:S(2)}) collective-permute-start(bf16[2,2,2,128,128]{4,3,2,1,0:T(8,128)(2,1)S(1)} %pad_maximum_fusion.rest_0_.rest_7_), channel_id=1, source_target_pairs={{0,8},{8,16},{16,24},{1,9},{9,17},{17,25},{2,10},{10,18},{18,26},{... | collective-permute-start | bytes 786440 | tf_op jit(solution)/shard_map/ppermute | solution.py:516
  7.6 12.2 %collective-permute-start.2 = (bf16[2,2,2,128,128]{4,3,2,1,0:T(8,128)(2,1)S(1)}, bf16[2,2,2,128,128]{4,3,2,1,0:T(8,128)(2,1)S(1)}, u32[]{:S(2)}, u32[]{:S(2)}) collective-permute-start(bf16[2,2,2,128,128]{4,3,2,1,0:T(8,128)(2,1)S(1)} %pad_maximum_fusion.rest_0_.rest_7_), channel_id=1, source_target_pairs={{0,2},{1,3},{2,0},{3,1},{4,6},{5,7},{6,4},{7,5},{8,10},{9,11},{10,... | collective-permute-start | bytes 786440 | tf_op jit(solution)/shard_map/ppermute | solution.py:510
  7.8 14.0 %collective-permute-start.1 = (bf16[2,2,2,128,128]{4,3,2,1,0:T(8,128)(2,1)S(1)}, bf16[2,2,2,128,128]{4,3,2,1,0:T(8,128)(2,1)S(1)}, u32[]{:S(2)}, u32[]{:S(2)}) collective-permute-start(bf16[2,2,2,128,128]{4,3,2,1,0:T(8,128)(2,1)S(1)} %pad_maximum_fusion.rest_0_.rest_7_), channel_id=1, source_target_pairs={{0,4},{1,5},{2,6},{3,7},{4,0},{5,1},{6,2},{7,3},{8,12},{9,13},{10,... | collective-permute-start | bytes 786440 | tf_op jit(solution)/shard_map/ppermute | solution.py:510
  10.5 0.6 copy-start.2
  11.1 12.0 %copy-start.3 = (s32[2,4]{1,0:T(2,128)}, s32[2,4]{1,0:T(2,128)S(1)}, u32[]{:S(2)}) copy-start(s32[2,4]{1,0:T(2,128)S(1)} %get-tuple-element.58.counts) | copy-start | bytes 100
  11.1 22.0 %copy-start.1 = (bf16[2,2,8,128,128]{4,3,2,1,0:T(8,128)(2,1)S(1)}, bf16[2,2,8,128,128]{4,3,2,1,0:T(8,128)(2,1)}, u32[]{:S(2)}) copy-start(bf16[2,2,8,128,128]{4,3,2,1,0:T(8,128)(2,1)} %get-tuple-element.59.own) | copy-start | bytes 3145732
  21.8 11.3 %collective-permute-start.6 = (bf16[2,2,2,128,128]{4,3,2,1,0:T(8,128)(2,1)S(1)}, bf16[2,2,2,128,128]{4,3,2,1,0:T(8,128)(2,1)S(1)}, u32[]{:S(2)}, u32[]{:S(2)}) collective-permute-start(bf16[2,2,2,128,128]{4,3,2,1,0:T(8,128)(2,1)S(1)} %collective-permute-done.1.rest_1_.rest_0_.rest_9_), channel_id=1, source_target_pairs={{0,2},{1,3},{2,0},{3,1},{4,6},{5,7},{6,4},{7,5},{8,10},{9,11},{10,... | collective-permute-start | bytes 786440 | tf_op jit(solution)/shard_map/ppermute | solution.py:510
  21.9 8.8 %collective-permute-start.5 = (bf16[2,2,2,128,128]{4,3,2,1,0:T(8,128)(2,1)S(1)}, bf16[2,2,2,128,128]{4,3,2,1,0:T(8,128)(2,1)S(1)}, u32[]{:S(2)}, u32[]{:S(2)}) collective-permute-start(bf16[2,2,2,128,128]{4,3,2,1,0:T(8,128)(2,1)S(1)} %collective-permute-done.1.rest_1_.rest_0_.rest_9_), channel_id=1, source_target_pairs={{0,8},{8,16},{16,24},{1,9},{9,17},{17,25},{2,10},{10,18},{18,26},{... | collective-permute-start | bytes 786440 | tf_op jit(solution)/shard_map/ppermute | solution.py:516
  30.6 8.1 %collective-permute-start.7 = (bf16[2,2,2,128,128]{4,3,2,1,0:T(8,128)(2,1)S(1)}, bf16[2,2,2,128,128]{4,3,2,1,0:T(8,128)(2,1)S(1)}, u32[]{:S(2)}, u32[]{:S(2)}) collective-permute-start(bf16[2,2,2,128,128]{4,3,2,1,0:T(8,128)(2,1)S(1)} %collective-permute-done.2.rest_1_.rest_8_), channel_id=1, source_target_pairs={{0,8},{8,16},{16,24},{1,9},{9,17},{17,25},{2,10},{10,18},{18,26},{... | collective-permute-start | bytes 786440 | tf_op jit(solution)/shard_map/ppermute | solution.py:516
  31.9 6.8 %collective-permute-start.8 = (bf16[2,2,2,128,128]{4,3,2,1,0:T(8,128)(2,1)S(1)}, bf16[2,2,2,128,128]{4,3,2,1,0:T(8,128)(2,1)S(1)}, u32[]{:S(2)}, u32[]{:S(2)}) collective-permute-start(bf16[2,2,2,128,128]{4,3,2,1,0:T(8,128)(2,1)S(1)} %collective-permute-done.5.rest_2_.rest_5_), channel_id=1, source_target_pairs={{0,2},{1,3},{2,0},{3,1},{4,6},{5,7},{6,4},{7,5},{8,10},{9,11},{10,... | collective-permute-start | bytes 786440 | tf_op jit(solution)/shard_map/ppermute | solution.py:510
  46.6 9.6 %collective-permute-start.9 = (bf16[2,2,2,128,128]{4,3,2,1,0:T(8,128)(2,1)S(1)}, bf16[2,2,2,128,128]{4,3,2,1,0:T(8,128)(2,1)S(1)}, u32[]{:S(2)}, u32[]{:S(2)}) collective-permute-start(bf16[2,2,2,128,128]{4,3,2,1,0:T(8,128)(2,1)S(1)} %get-tuple-element.66), channel_id=1, source_target_pairs={{0,2},{1,3},{2,0},{3,1},{4,6},{5,7},{6,4},{7,5},{8,10},{9,11},{10,... | collective-permute-start | bytes 786440 | tf_op jit(solution)/shard_map/ppermute | solution.py:510
  47.7 23.6 %collective-permute-start.12 = (bf16[4,2,2,128,128]{4,3,2,1,0:T(8,128)(2,1)S(1)}, bf16[4,2,2,128,128]{4,3,2,1,0:T(8,128)(2,1)S(1)}, u32[]{:S(2)}, u32[]{:S(2)}) collective-permute-start(bf16[4,2,2,128,128]{4,3,2,1,0:T(8,128)(2,1)S(1)} %get-tuple-element.83), channel_id=1, source_target_pairs={{8,0},{16,8},{24,16},{9,1},{17,9},{25,17},{10,2},{18,10},{26,18},{... | collective-permute-start | bytes 1572872 | tf_op jit(solution)/shard_map/ppermute | solution.py:519
  56.3 16.4 %copy-start = (f32[320,128]{1,0:T(8,128)S(1)}, f32[320,128]{1,0:T(8,128)}, u32[]{:S(2)}) copy-start(f32[320,128]{1,0:T(8,128)} %constant.2.clone.refs_4_.rest_11_.rest_4_) | copy-start | bytes 491524
  56.3 10.2 %collective-permute-start.10 = (bf16[2,2,2,128,128]{4,3,2,1,0:T(8,128)(2,1)S(1)}, bf16[2,2,2,128,128]{4,3,2,1,0:T(8,128)(2,1)S(1)}, u32[]{:S(2)}, u32[]{:S(2)}) collective-permute-start(bf16[2,2,2,128,128]{4,3,2,1,0:T(8,128)(2,1)S(1)} %add_convert_fusion.2), channel_id=1, source_target_pairs={{8,0},{16,8},{24,16},{9,1},{17,9},{25,17},{10,2},{18,10},{26,18},{... | collective-permute-start | bytes 786440 | tf_op jit(solution)/shard_map/ppermute | solution.py:519
  60.5 6.0 %collective-permute-start.11 = (bf16[2,2,2,128,128]{4,3,2,1,0:T(8,128)(2,1)S(1)}, bf16[2,2,2,128,128]{4,3,2,1,0:T(8,128)(2,1)S(1)}, u32[]{:S(2)}, u32[]{:S(2)}) collective-permute-start(bf16[2,2,2,128,128]{4,3,2,1,0:T(8,128)(2,1)S(1)} %get-tuple-element.74), channel_id=1, source_target_pairs={{0,2},{1,3},{2,0},{3,1},{4,6},{5,7},{6,4},{7,5},{8,10},{9,11},{10,... | collective-permute-start | bytes 786440 | tf_op jit(solution)/shard_map/ppermute | solution.py:510
  66.6 25.6 %collective-permute-start.16 = (bf16[2,2,2,128,128]{4,3,2,1,0:T(8,128)(2,1)S(1)}, bf16[2,2,2,128,128]{4,3,2,1,0:T(8,128)(2,1)S(1)}, u32[]{:S(2)}, u32[]{:S(2)}) collective-permute-start(bf16[2,2,2,128,128]{4,3,2,1,0:T(8,128)(2,1)S(1)} %add_convert_fusion.1), channel_id=1, source_target_pairs={{0,4},{1,5},{2,6},{3,7},{4,0},{5,1},{6,2},{7,3},{8,12},{9,13},{10,... | collective-permute-start | bytes 786440 | tf_op jit(solution)/shard_map/ppermute | solution.py:510
  71.4 20.7 %collective-permute-start.15 = (bf16[2,2,2,128,128]{4,3,2,1,0:T(8,128)(2,1)S(1)}, bf16[2,2,2,128,128]{4,3,2,1,0:T(8,128)(2,1)S(1)}, u32[]{:S(2)}, u32[]{:S(2)}) collective-permute-start(bf16[2,2,2,128,128]{4,3,2,1,0:T(8,128)(2,1)S(1)} %add_convert_fusion), channel_id=1, source_target_pairs={{0,2},{1,3},{2,0},{3,1},{4,6},{5,7},{6,4},{7,5},{8,10},{9,11},{10,... | collective-permute-start | bytes 786440 | tf_op jit(solution)/shard_map/ppermute | solution.py:510
  81.2 13.2 %collective-permute-start.13 = (bf16[2,128,1024]{2,1,0:T(8,128)(2,1)S(1)}, bf16[2,128,1024]{2,1,0:T(8,128)(2,1)S(1)}, u32[]{:S(2)}, u32[]{:S(2)}) collective-permute-start(bf16[2,128,1024]{2,1,0:T(8,128)(2,1)S(1)} %get-tuple-element.89), channel_id=1, source_target_pairs={{0,1},{1,0},{2,3},{3,2},{4,5},{5,4},{6,7},{7,6},{8,9},{9,8},{10,11... | collective-permute-start | bytes 1572872 | tf_op jit(solution)/shard_map/ppermute | solution.py:510
  92.0 2.5 %collective-permute-start.14 = (bf16[2,128,1024]{2,1,0:T(8,128)(2,1)S(1)}, bf16[2,128,1024]{2,1,0:T(8,128)(2,1)S(1)}, u32[]{:S(2)}, u32[]{:S(2)}) collective-permute-start(bf16[2,128,1024]{2,1,0:T(8,128)(2,1)S(1)} %get-tuple-element.90), channel_id=1, source_target_pairs={{0,1},{1,0},{2,3},{3,2},{4,5},{5,4},{6,7},{7,6},{8,9},{9,8},{10,11... | collective-permute-start | bytes 1572872 | tf_op jit(solution)/shard_map/ppermute | solution.py:510
  93.0 1.5 %collective-permute-start.17 = (bf16[2,128,256]{2,1,0:T(8,128)(2,1)S(1)}, bf16[2,128,256]{2,1,0:T(8,128)(2,1)S(1)}, u32[]{:S(2)}, u32[]{:S(2)}) collective-permute-start(bf16[2,128,256]{2,1,0:T(8,128)(2,1)S(1)} %get-tuple-element.95), channel_id=1, source_target_pairs={{0,1},{1,0},{2,3},{3,2},{4,5},{5,4},{6,7},{7,6},{8,9},{9,8},{10,11... | collective-permute-start | bytes 393224 | tf_op jit(solution)/shard_map/ppermute | solution.py:510
